TPU v7x, 32 devices: a whole 2x2x4 slice. The times are simulated.
32 devices in a mesh: frame: 4 (over x, core), row: 4 (over z), col: 2 (over y).
Axes of the slice: x: 2, y: 2, z: 4, core: 2. Of those that a mesh axis runs over, the one named last changes fastest.
Arguments:
- queries: bfloat16 [8, 32, 16, 2240], P('frame', 'row', 'col'), may hold values from -5 to 5
- keys: bfloat16 [8, 32, 16, 2240], P('frame', 'row', 'col'), may hold values from -120 to 120
- values: bfloat16 [8, 32, 16, 2240], P('frame', 'row', 'col'), may hold values from -12 to 12
- hidden: bfloat16 [8, 32, 16, 5632], P('frame', 'row', 'col'), may hold values from -5 to 5
- conv_weight: float32 [9, 5632], replicated, may hold values from -2 to 2
- conv_bias: float32 [5632], replicated, may hold values from -2.5 to 2.5
Outputs:
- attended: bfloat16 [8, 32, 16, 2240], P('frame', 'row', 'col')
- gated: bfloat16 [8, 32, 16, 2816], P('frame', 'row', 'col')
All inputs are finite; a program needn't handle non-finite values.
Results may differ from a plain program's by a relative error of at most 0.0004.
Values may be sent and summed in bfloat16 or wider, within the bound.
No kernel may reach another device: no remote copies, remote signals or barrier semaphores. Data moves between devices by JAX's collectives and lax.ppermute only.
A program may use at most 64 MiB of HBM per device.

v0:
```python
import jax
import jax.numpy as jnp
from jax import lax
from jax.sharding import PartitionSpec as P

HEADS = 70
HD = 32


EPS = 1e-06
HIGH = lax.Precision.HIGHEST


def carried_in(value, axis, join, neutral):
    count, mine = (lax.axis_size(axis), lax.axis_index(axis))
    pieces = jax.tree.map(lambda part: lax.all_gather(part, axis), value)
    running = jax.tree.map(
        lambda part, zero: jnp.full_like(part, 0) + jnp.asarray(zero, part.dtype), value, neutral
    )

    def lap(position, running):
        longer = join(running, jax.tree.map(lambda part: part[position], pieces))
        return jax.tree.map(lambda new, old: jnp.where(position < mine, new, old), longer, running)

    return lax.fori_loop(0, count - 1, lap, running)


def extended(value, sides, width):
    for axis, dim in sides:
        peers, length = (lax.axis_size(axis), value.shape[dim])
        up = [(i, (i + 1) % peers) for i in range(peers - 1)]
        down = [(j, i) for i, j in up]
        last = lax.slice_in_dim(value, length - width, length, axis=dim)
        initial = lax.slice_in_dim(value, 0, width, axis=dim)
        before = lax.ppermute(last, axis, up)
        after = lax.ppermute(initial, axis, down)
        value = jnp.concatenate([before, value, after], axis=dim)
    return value


def add_pairs(earlier, later):
    return (earlier[0] + later[0], earlier[1] + later[1])


def over_space(pair):
    return lax.psum((pair[0], pair[1]), ("row", "col"))


def earlier_frames(pair):
    identity = (jnp.zeros_like(pair[0]), jnp.zeros_like(pair[1]))
    return carried_in(pair, "frame", add_pairs, identity)


def on_device(queries, keys, values, hidden, conv_weight, conv_bias):
    kpos = jnp.maximum(keys, 0).reshape(-1, HEADS, HD)
    vals = values.reshape(-1, HEADS, HD)
    local_state = jnp.einsum("thd,the->hde", kpos, vals, preferred_element_type=jnp.float32)
    local_ksum = jnp.sum(kpos.astype(jnp.float32), axis=0)
    spatial = over_space((local_state, local_ksum))
    before = earlier_frames(spatial)
    total_state = before[0] + spatial[0]
    total_ksum = before[1] + spatial[1]
    qpos = jnp.maximum(queries, 0).astype(jnp.float32).reshape(-1, HEADS, HD)
    numer = jnp.einsum("thd,hde->the", qpos, total_state, precision=HIGH)
    denom = jnp.einsum("thd,hd->th", qpos, total_ksum, precision=HIGH) + EPS
    attended = (numer / denom[..., None]).reshape(queries.shape).astype(jnp.bfloat16)
    padded = extended(hidden, (("row", 1), ("col", 2)), 1)
    frames, tile_rows, tile_cols, channels = hidden.shape
    total = jnp.zeros((frames, tile_rows, tile_cols, channels), jnp.float32) + conv_bias
    for shift_r in range(3):
        for shift_c in range(3):
            window = padded[:, shift_r : shift_r + tile_rows, shift_c : shift_c + tile_cols]
            total = total + conv_weight[3 * shift_r + shift_c] * window.astype(jnp.float32)
    half = channels // 2
    gated = (total[..., :half] * jax.nn.silu(total[..., half:])).astype(jnp.bfloat16)
    return (attended, gated)


def solution(mesh):
    placed = (
        P("frame", "row", "col", None),
        P("frame", "row", "col", None),
        P("frame", "row", "col", None),
        P("frame", "row", "col", None),
        P(),
        P(),
    )
    return jax.shard_map(
        on_device,
        mesh=mesh,
        in_specs=placed,
        out_specs=(P("frame", "row", "col", None), P("frame", "row", "col", None)),
        check_vma=False,
    )
```

profile of v0, /device:TPU:0, one launch (start us, length us, event | category | flops | bytes accessed | tf_op | source)
XLA Modules:
  0.0 168.1 jit_solution(15172907788477132361)
XLA Ops:
  7.2 0.0 all-reduce.2.cloned.1.call-start
  7.2 1.7 %fusion.10 = (bf16[2,1,8,5632]{3,2,1,0:T(8,128)(2,1)}, bf16[2,1,8,5632]{3,2,1,0:T(8,128)(2,1)S(1)}) fusion(bf16[2,8,8,5632]{3,2,1,0:T(8,128)(2,1)} %param.11), kind=kLoop, calls=%fused_computation.37 | loop fusion | bytes 720896 | tf_op jit(solution)/shard_map/slice | solution.py:33
  8.9 4.9 %collective-permute-start = (bf16[2,1,8,5632]{3,2,1,0:T(8,128)(2,1)}, bf16[2,1,8,5632]{3,2,1,0:T(8,128)(2,1)S(1)}, u32[]{:S(2)}, u32[]{:S(2)}) collective-permute-start(bf16[2,1,8,5632]{3,2,1,0:T(8,128)(2,1)} %get-tuple-element.178), channel_id=1, source_target_pairs={{0,2},{2,4},{4,6},{1,3},{3,5},{5,7},{8,10},{10,12},{12,14},{9,11},... | collective-permute-start | bytes 540680 | tf_op jit(solution)/shard_map/ppermute | solution.py:35
  13.8 1.3 collective-permute-start.1
  15.1 1.1 broadcast_maximum_fusion.1
  16.3 2.0 %reshape.27 = bf16[128,70,32]{2,1,0:T(8,128)(2,1)S(1)} reshape(bf16[2,8,8,2240]{3,2,1,0:T(8,128)(2,1)S(1)} %broadcast_maximum_fusion.1) | data formatting | bytes 1146880 | tf_op jit(solution)/shard_map/reshape | solution.py:55
  18.2 4.2 %reshape.28 = bf16[128,70,32]{2,1,0:T(8,128)(2,1)} reshape(bf16[2,8,8,2240]{3,2,1,0:T(8,128)(2,1)} %param.10) | data formatting | bytes 1146880 | tf_op jit(solution)/shard_map/reshape | solution.py:56
  22.4 3.5 %fusion = f32[70,32,32]{2,1,0:T(8,128)} fusion(bf16[128,70,32]{2,1,0:T(8,128)(2,1)} %reshape.28, bf16[128,70,32]{2,1,0:T(8,128)(2,1)S(1)} %reshape.27), kind=kOutput, calls=%fused_computation.6 | convolution fusion | flops 18350080 | bytes 1433600 | tf_op jit(solution)/shard_map/thd,the->hde/dot_general | solution.py:57
  25.9 0.0 all-reduce.2.cloned.1.call-update
  25.9 0.0 all-gather.5.cloned.1.call-start
  26.0 0.9 broadcast_maximum_fusion
  26.8 1.8 %copy.40 = bf16[2,8,8,5632]{3,1,2,0:T(8,128)(2,1)S(1)} copy(bf16[2,8,8,5632]{3,2,1,0:T(8,128)(2,1)} %param.11) | data formatting | bytes 2883584 | tf_op args[3]
  28.7 0.0 collective-permute-done
  28.7 0.3 copy.39
  29.0 0.0 collective-permute-done.1
  29.0 0.3 copy.41
  29.3 1.2 pad_maximum_fusion.5
  30.5 4.2 %collective-permute-start.2 = (bf16[2,10,1,5632]{3,1,2,0:T(8,128)(2,1)}, bf16[2,10,1,5632]{3,1,2,0:T(8,128)(2,1)}, u32[]{:S(2)}, u32[]{:S(2)}) collective-permute-start(bf16[2,10,1,5632]{3,1,2,0:T(8,128)(2,1)} %get-tuple-element.176), channel_id=1, source_target_pairs={{0,1},{2,3},{4,5},{6,7},{8,9},{10,11},{12,13},{14,15},{16,17},{18,... | collective-permute-start | bytes 675848 | tf_op jit(solution)/shard_map/ppermute | solution.py:35
  34.6 1.3 collective-permute-start.3
  35.9 0.1 convert_reduce_fusion
  36.1 0.1 reduce_sum.12
  36.1 40.8 %psum.15 = f32[70,32]{1,0:T(8,128)S(1)} all-reduce(f32[70,32]{1,0:T(8,128)S(1)} %reduce_sum.12), channel_id=1, replica_groups=mesh['frame'=4,'row'=4,'col'=2] {'row','col'}, use_global_device_ids=true, to_apply=%region_2.0 | all-reduce | flops 2240 | bytes 17920 | tf_op jit(solution)/shard_map/psum | solution.py:46
  76.9 0.1 copy.34
  77.0 4.2 %reshape.29 = bf16[128,70,32]{2,1,0:T(8,128)(2,1)} reshape(bf16[2,8,8,2240]{3,2,1,0:T(8,128)(2,1)} %broadcast_maximum_fusion) | data formatting | bytes 1146880 | tf_op jit(solution)/shard_map/reshape | solution.py:63
  81.2 3.8 %copy.37 = bf16[128,70,32]{0,2,1:T(8,128)(2,1)} copy(bf16[128,70,32]{2,1,0:T(8,128)(2,1)} %reshape.29) | data formatting | bytes 1146880 | tf_op jit(solution)/shard_map/reshape | solution.py:63
  85.0 5.4 %all-gather.2 = f32[4,70,32]{1,2,0:T(8,128)S(1)} all-gather(f32[1,70,32]{1,2,0:T(8,128)S(1)} %copy.34), channel_id=3, replica_groups=mesh['frame'=4,'row'=4,'col'=2] {'frame'}, dimensions={0}, use_global_device_ids=true | all-gather | bytes 44800 | tf_op jit(solution)/shard_map/all_gather | solution.py:16
  90.4 3.0 %slice_reduce_fusion.8 = (f32[5632]{0:T(1024)S(1)}, f32[5632]{0:T(1024)S(1)}, f32[5632]{0:T(1024)S(1)}, f32[5632]{0:T(1024)S(1)}, f32[5632]{0:T(1024)}, /*index=...) fusion(f32[9,5632]{1,0:T(8,128)} %param.12), kind=kLoop, calls=%fused_computation.36 | loop fusion | bytes 405504 | tf_op jit(solution)/shard_map/slice | solution.py:73
  93.4 16.9 %all-reduce.2.cloned.1.call-done = f32[70,32,32]{2,1,0:T(8,128)} async-done(((f32[70,32,32]{2,1,0:T(8,128)}), f32[70,32,32]{2,1,0:T(8,128)}) %all-reduce.2.cloned.1.call-update) | async-done | bytes 286736 | tf_op jit(solution)/shard_map/psum | solution.py:46
  110.3 0.0 all-gather.5.cloned.1.call-update
  110.3 0.0 copy-start.9
  110.4 0.0 collective-permute-done.2
  110.4 0.0 collective-permute-done.3
  110.4 5.1 %maximum_maximum_fusion = (bf16[2,10,9,5632]{3,1,2,0:T(8,128)(2,1)S(1)}, bf16[2,10,9,5632]{3,1,2,0:T(8,128)(2,1)S(1)}) fusion(bf16[2,1,8,5632]{3,1,2,0:T(2,128)(2,1)S(1)} %copy.41, bf16[2,8,8,5632]{3,1,2,0:T(8,128)(2,1)S(1)} %copy.40, bf16[2,1,8,5632]{3,1,2,0:T(2,128)(2,1)S(1)} %copy.39, bf16[2,10,1,5632]{3,1,2,0:T(8,128)(2,1)} %collective-permute-done.2, ...), kind=kLoop, calls=%fused_computation.3 | loop fusion | flops 16220160 | bytes 6307840 | tf_op jit(solution)/shard_map/concatenate | solution.py:37
  115.5 4.1 %multiply_add_fusion = f32[2,8,8,5632]{3,1,2,0:T(8,128)S(1)} fusion(bf16[2,8,8,5632]{3,1,2,0:T(8,128)(2,1)S(1)} %copy.40, bf16[2,10,9,5632]{3,1,2,0:T(8,128)(2,1)S(1)} %get-tuple-element.175, bf16[2,1,8,5632]{3,1,2,0:T(2,128)(2,1)S(1)} %copy.41, bf16[2,10,9,5632]{3,1,2,0:T(8,128)(2,1)S(1)} %get-tuple-element.174, bf16[2,1,8,5632]{3,1,2,0:T(2,128)(2,1)S(1)} %copy.39, ...), kind=kLoop, calls=%fused_computation.5 | loop fusion | flops 23789568 | bytes 13561856 | tf_op jit(solution)/shard_map/add | solution.py:73
  119.6 0.4 fusion.3
  120.0 1.0 copy.47
  121.0 27.2 %all-gather.5.cloned.1.call-done = f32[280,32,32]{2,1,0:T(8,128)} async-done(((f32[70,32,32]{2,1,0:T(8,128)}), f32[280,32,32]{2,1,0:T(8,128)}) %all-gather.5.cloned.1.call-update) | async-done | bytes 1146896 | tf_op jit(solution)/shard_map/all_gather | solution.py:16
  148.3 5.5 %while.16 = (s32[]{:T(128)}, f32[70,32,32]{2,1,0:T(8,128)S(1)}, f32[70,32]{1,0:T(8,128)S(1)}, s32[]{:T(128)}, f32[4,70,32,32]{3,2,1,0:T(8,128)}, /*index=5*/f32[4,70,32]{1,2,0:T(8,128)S(1)}, s32[]{:T(128)}, s32[]{:T(128)}) while((s32[]{:T(128)}, f32[70,32,32]{2,1,0:T(8,128)S(1)}, f32[70,32]{1,0:T(8,128)S(1)}, s32[]{:T(128)}, ...), condition=%wide.region_4.5_spmd.clone, body=%wide.region_3.4_spmd.clone.sunk | while | flops 221764 | bytes 922995 | solution.py:25
  148.3 1.8 %add_select_fusion.4 = f32[70,32,32]{2,1,0:T(8,128)S(1)} fusion(f32[70,32,32]{2,1,0:T(8,128)S(1)} %get-tuple-element.226, f32[4,70,32,32]{3,2,1,0:T(8,128)} %get-tuple-element.237, s32[]{:T(128)} %get-tuple-element.225, pred[]{:T(512)S(6)} %compare.3, pred[]{:T(512)S(6)} %lt.23), kind=kLoop, calls=%fused_computation.clone.1 | loop fusion | flops 215040 | bytes 860166 | tf_op jit(solution)/shard_map/while/body/eval_jaxpr/jit(_where)/select_n | solution.py:23
  150.1 0.1 copy.60
  150.2 1.7 add_select_fusion.4
  151.9 0.1 copy.60
  152.0 1.7 add_select_fusion.4
  153.7 0.1 copy.60
  153.8 0.6 fusion.8
  154.4 1.9 %fusion.5 = bf16[128,70,32]{0,2,1:T(8,128)(2,1)} fusion(bf16[128,70,32]{0,2,1:T(8,128)(2,1)S(1)} %copy-done.3, f32[70,32,32]{2,1,0:T(8,128)S(1)} %get-tuple-element.112, f32[70,32,32]{2,1,0:T(8,128)S(1)} %copy-done.1, f32[128,70]{0,1:T(8,128)S(1)} %fusion.7), kind=kOutput, calls=%fused_computation.15 | convolution fusion | flops 110745600 | bytes 1756160 | tf_op jit(solution)/shard_map/thd,hde->the/dot_general | solution.py:64
  156.3 2.7 %copy.38 = bf16[128,70,32]{2,1,0:T(8,128)(2,1)S(1)} copy(bf16[128,70,32]{0,2,1:T(8,128)(2,1)} %fusion.5) | data formatting | bytes 1146880 | tf_op jit(solution)/shard_map/convert_element_type | solution.py:66
  159.1 2.1 %convert_element_type.43 = bf16[2,8,8,2240]{3,2,1,0:T(8,128)(2,1)} reshape(bf16[128,70,32]{2,1,0:T(8,128)(2,1)S(1)} %copy.38) | data formatting | bytes 1146880 | tf_op jit(solution)/shard_map/convert_element_type | solution.py:66
  (29 shorter events, 0.1 us)
Async XLA Ops:
  7.2 103.1 %all-reduce.2.cloned.1.call-start = ((), (), s32[]{:S(2)}) async-start(), calls=%async_computation | async-start | bytes 2293760 | tf_op jit(solution)/shard_map/psum | solution.py:46
  8.9 19.8 %collective-permute-start = (bf16[2,1,8,5632]{3,2,1,0:T(8,128)(2,1)}, bf16[2,1,8,5632]{3,2,1,0:T(8,128)(2,1)S(1)}, u32[]{:S(2)}, u32[]{:S(2)}) collective-permute-start(bf16[2,1,8,5632]{3,2,1,0:T(8,128)(2,1)} %get-tuple-element.178), channel_id=1, source_target_pairs={{0,2},{2,4},{4,6},{1,3},{3,5},{5,7},{8,10},{10,12},{12,14},{9,11},... | collective-permute-start | bytes 540680 | tf_op jit(solution)/shard_map/ppermute | solution.py:35
  13.8 15.1 %collective-permute-start.1 = (bf16[2,1,8,5632]{3,2,1,0:T(8,128)(2,1)S(1)}, bf16[2,1,8,5632]{3,2,1,0:T(8,128)(2,1)S(1)}, u32[]{:S(2)}, u32[]{:S(2)}) collective-permute-start(bf16[2,1,8,5632]{3,2,1,0:T(8,128)(2,1)S(1)} %get-tuple-element.179), channel_id=1, source_target_pairs={{2,0},{4,2},{6,4},{3,1},{5,3},{7,5},{10,8},{12,10},{14,12},{11,9},... | collective-permute-start | bytes 540680 | tf_op jit(solution)/shard_map/ppermute | solution.py:36
  22.4 3.6 %copy-start.2 = (bf16[2,8,8,2240]{3,2,1,0:T(8,128)(2,1)S(1)}, bf16[2,8,8,2240]{3,2,1,0:T(8,128)(2,1)}, u32[]{:S(2)}) copy-start(bf16[2,8,8,2240]{3,2,1,0:T(8,128)(2,1)} %param.8) | copy-start | bytes 1720324
  25.9 122.4 %all-gather.5.cloned.1.call-start = ((), (), s32[]{:S(2)}) async-start(), calls=%async_computation.1 | async-start | bytes 5734400 | tf_op jit(solution)/shard_map/all_gather | solution.py:16
  26.8 9.1 %copy-start = (bf16[2,8,8,2240]{3,2,1,0:T(8,128)(2,1)S(1)}, bf16[2,8,8,2240]{3,2,1,0:T(8,128)(2,1)}, u32[]{:S(2)}) copy-start(bf16[2,8,8,2240]{3,2,1,0:T(8,128)(2,1)} %param.9) | copy-start | bytes 1720324
  30.5 79.9 %collective-permute-start.2 = (bf16[2,10,1,5632]{3,1,2,0:T(8,128)(2,1)}, bf16[2,10,1,5632]{3,1,2,0:T(8,128)(2,1)}, u32[]{:S(2)}, u32[]{:S(2)}) collective-permute-start(bf16[2,10,1,5632]{3,1,2,0:T(8,128)(2,1)} %get-tuple-element.176), channel_id=1, source_target_pairs={{0,1},{2,3},{4,5},{6,7},{8,9},{10,11},{12,13},{14,15},{16,17},{18,... | collective-permute-start | bytes 675848 | tf_op jit(solution)/shard_map/ppermute | solution.py:35
  34.6 75.8 %collective-permute-start.3 = (bf16[2,10,1,5632]{3,1,2,0:T(8,128)(2,1)}, bf16[2,10,1,5632]{3,1,2,0:T(8,128)(2,1)}, u32[]{:S(2)}, u32[]{:S(2)}) collective-permute-start(bf16[2,10,1,5632]{3,1,2,0:T(8,128)(2,1)} %get-tuple-element.177), channel_id=1, source_target_pairs={{1,0},{3,2},{5,4},{7,6},{9,8},{11,10},{13,12},{15,14},{17,16},{19,... | collective-permute-start | bytes 675848 | tf_op jit(solution)/shard_map/ppermute | solution.py:36
  110.3 5.1 %copy-start.4 = (f32[5632]{0:T(1024)S(1)}, f32[5632]{0:T(1024)}, u32[]{:S(2)}) copy-start(f32[5632]{0:T(1024)} %get-tuple-element.157) | copy-start | bytes 67588
  110.3 5.1 %copy-start.5 = (f32[5632]{0:T(1024)S(1)}, f32[5632]{0:T(1024)}, u32[]{:S(2)}) copy-start(f32[5632]{0:T(1024)} %get-tuple-element.158) | copy-start | bytes 67588
  110.3 5.1 %copy-start.6 = (f32[5632]{0:T(1024)S(1)}, f32[5632]{0:T(1024)}, u32[]{:S(2)}) copy-start(f32[5632]{0:T(1024)} %get-tuple-element.159) | copy-start | bytes 67588
  110.3 5.1 %copy-start.7 = (f32[5632]{0:T(1024)S(1)}, f32[5632]{0:T(1024)}, u32[]{:S(2)}) copy-start(f32[5632]{0:T(1024)} %get-tuple-element.160) | copy-start | bytes 67588
  110.3 5.1 %copy-start.8 = (f32[5632]{0:T(1024)S(1)}, f32[5632]{0:T(1024)}, u32[]{:S(2)}) copy-start(f32[5632]{0:T(1024)} %get-tuple-element.161) | copy-start | bytes 67588
  110.3 5.1 %copy-start.9 = (f32[5632]{0:T(1024)S(1)}, f32[5632]{0:T(1024)}, u32[]{:S(2)}) copy-start(f32[5632]{0:T(1024)} %param.13) | copy-start | bytes 67588
  148.3 5.6 %copy-start.3 = (bf16[128,70,32]{0,2,1:T(8,128)(2,1)S(1)}, bf16[128,70,32]{0,2,1:T(8,128)(2,1)}, u32[]{:S(2)}) copy-start(bf16[128,70,32]{0,2,1:T(8,128)(2,1)} %copy.37) | copy-start | bytes 1720324
  148.3 6.1 %copy-start.1 = (f32[70,32,32]{2,1,0:T(8,128)S(1)}, f32[70,32,32]{2,1,0:T(8,128)}, u32[]{:S(2)}) copy-start(f32[70,32,32]{2,1,0:T(8,128)} %all-reduce.2.cloned.1.call-done) | copy-start | bytes 860164
Sparse Core Ops, SparseCore 0:
  26.0 84.2 all-reduce.1
  111.9 36.3 all-gather.4
where the time goes:
time: 169 us; the launch traced here: 168 us
  blocking collectives  46.2 us (27%)
  waiting for transfers between devices  44.2 us (26%)
  local copies, waits for them, and re-layouts  27.5 us (16%)
  other arithmetic  18 us (11%)
  between operations  14.3 us (8%)
  starting transfers between devices  11.7 us (7%)
  matrix products  6 us (4%)
    psum x1, blocking collectives, over_space(): return lax.psum((pair[0], pair[1]), ('row', 'col'))  40.8 us
    all_gather x1, waiting for transfers between devices, carried_in(): pieces = jax.tree.map(lambda part: lax.all_gather(part, axis), value)  27.2 us
    psum x1, waiting for transfers between devices, over_space(): return lax.psum((pair[0], pair[1]), ('row', 'col'))  16.9 us
    ppermute x2, starting transfers between devices, extended(): before = lax.ppermute(last, axis, up)  9.08 us
    reshape x2, local copies, waits for them, and re-layouts, on_device(): qpos = jnp.maximum(queries, 0).astype(jnp.float32).reshape(-1, HEADS, HD)  7.94 us
    all_gather x1, blocking collectives, carried_in(): pieces = jax.tree.map(lambda part: lax.all_gather(part, axis), value)  5.41 us
    select_n x6, other arithmetic, lap(): jnp.where(position < mine, new, old)  5.12 us
    concatenate x1, other arithmetic, extended(): value = jnp.concatenate([before, value, after], axis=dim)  5.06 us
  transfers between devices with their start and end apart: 6, of which 2 were waited for; matrix products, arithmetic and copies ran while one was open for 22% of the time, Pallas kernels for 0%

commit v1 on v0

v1 whole, which is shorter than its diff:
```python
import functools

import jax
import jax.numpy as jnp
from jax import lax
from jax.experimental import pallas as pl
from jax.experimental.pallas import tpu as pltpu
from jax.sharding import PartitionSpec as P

HEADS = 70
HD = 32
EPS = 1e-06
LANE = 128
F32 = jnp.float32
BF16 = jnp.bfloat16
VMEM_LIMIT = 40 * 1024 * 1024
VMEM_MOST = 60 * 1024 * 1024


def whole(n):
    return [pl.BlockSpec(memory_space=pltpu.VMEM)] * n


def lane_tiles(width):
    return -(-width // LANE)


def piece_rows(width, pieces):
    return 8 * -(-lane_tiles(width) * (HD + 1) // (8 * pieces))


def target(place, step, n):
    return place ^ step if n & (n - 1) == 0 else (place + step) % n


def source(place, step, n):
    return place ^ step if n & (n - 1) == 0 else (place + n - step) % n


def piece(place, per):
    return pl.ds(pl.multiple_of(place * per, 8), per)


def same_head(shape):
    first = lax.broadcasted_iota(jnp.int32, shape, 0) // HD
    second = lax.broadcasted_iota(jnp.int32, shape, 1) // HD
    return first == second


def state_kernel(width, pieces, keys, values, *refs):
    *outs, k_ref, v_ref, held, sems = refs
    tokens = k_ref.shape[0]
    tiles = lane_tiles(width)
    half = tiles // 2
    loads = []
    for c, (lo, hi) in enumerate(((0, half * LANE), (half * LANE, width))):
        at = pl.ds(lo, hi - lo)
        for i, (array, ref) in enumerate(((keys, k_ref), (values, v_ref))):
            loads.append(pltpu.make_async_copy(array.at[:, at], ref.at[:, at], sems.at[c, i]))
            loads[-1].start()
    ones = jnp.ones((8, tokens), BF16)
    held[tiles * HD :, :] = jnp.zeros((held.shape[0] - tiles * HD, LANE), F32)
    for j in range(tiles):
        if j in (0, half):
            for copy in loads[2 * (j // half) : 2 * (j // half) + 2]:
                copy.wait()
        lo, hi = j * LANE, min(width, (j + 1) * LANE)
        n = hi - lo
        kpos = jnp.maximum(k_ref[:, lo:hi], 0)
        vals = v_ref[:, lo:hi]
        full = lax.dot_general(kpos, vals, (((0,), (0,)), ((), ())), preferred_element_type=F32)
        ksum = jnp.dot(ones, kpos, preferred_element_type=F32)
        head = lax.broadcasted_iota(jnp.int32, (HD, n), 1) // HD
        packed = jnp.zeros((HD, n), F32)
        for i in range(n // HD):
            packed = jnp.where(head == i, full[i * HD : (i + 1) * HD, :], packed)
        if n < LANE:
            held[j * HD : (j + 1) * HD, :] = jnp.zeros((HD, LANE), F32)
        held[j * HD : (j + 1) * HD, :n] = packed
        held[tiles * HD + j : tiles * HD + j + 1, :n] = ksum[:1]
    mine = lax.axis_index(GROUP)
    for step, out in enumerate(outs):
        rows = piece(target(mine, step, pieces), 8 * out.shape[0])
        out[...] = held[rows, :].reshape(out.shape)


def halves(x):
    high = x.astype(BF16)
    return high, (x - high.astype(F32)).astype(BF16)


def attend_kernel(width, q_ref, *refs):
    *quarters, out, p_ref, out_ref, sems = refs
    mine, pieces = lax.axis_index(GROUP), len(quarters)
    for step, quarter in enumerate(quarters):
        rows = piece(source(mine, step, pieces), 8 * quarter.shape[0])
        p_ref[rows, :] = quarter[...].reshape(-1, LANE)
    tiles = lane_tiles(width)
    parts = sems.shape[0]
    firsts = [tiles * c // parts for c in range(parts + 1)]
    stores = []
    for j in range(tiles):
        lo, hi = j * LANE, min(width, (j + 1) * LANE)
        n = hi - lo
        qpos = jnp.maximum(q_ref[:, lo:hi], 0)
        same = same_head((n, n))
        part = p_ref[j * HD : (j + 1) * HD, :n]
        spread = jnp.where(same, jnp.concatenate([part] * (n // HD), axis=0), 0.0)
        zrow = p_ref[tiles * HD + j : tiles * HD + j + 1, :n]
        block = same.astype(F32).astype(BF16)
        numer = jnp.dot(
            jnp.concatenate([qpos, qpos], axis=1),
            jnp.concatenate(halves(spread), axis=0),
            preferred_element_type=F32,
        )
        denom = jnp.dot(
            jnp.concatenate(halves(qpos.astype(F32) * zrow), axis=1),
            jnp.concatenate([block, block], axis=0),
            preferred_element_type=F32,
        )
        out_ref[:, lo:hi] = (numer / (denom + EPS)).astype(BF16)
        if j + 1 in firsts:
            c = firsts.index(j + 1) - 1
            at = pl.ds(firsts[c] * LANE, hi - firsts[c] * LANE)
            stores.append(pltpu.make_async_copy(out_ref.at[:, at], out.at[:, at], sems.at[c]))
            stores[-1].start()
    for copy in stores:
        copy.wait()


def place(axis):
    return lax.axis_index(axis), lax.axis_size(axis)


def chosen(by_even, by_odd, mine, n):
    if n == 1:
        return jnp.zeros_like(by_even), jnp.zeros_like(by_even)
    if n == 2:
        return jnp.where(mine == 1, by_even, 0), jnp.where(mine == 0, by_even, 0)
    is_even = lax.rem(mine, 2) == 0
    before = jnp.where(is_even, by_odd, by_even)
    after = jnp.where(is_even, by_even, by_odd)
    return jnp.where(mine == 0, 0, before), jnp.where(mine == n - 1, 0, after)


def conv_kernel(hidden, row_e, row_o, col_e, col_o, weight, bias, out, held, sems):
    frames, rows, cols, channels = hidden.shape
    half = channels // 2
    in_rows, (col, n_cols) = place(ROW), place("col")
    steps, parts = half // LANE, sems.shape[0]

    def conv(f, i):
        at = pl.ds(pl.multiple_of(i * LANE, LANE), LANE)
        w = weight[:, at]
        spot = lax.broadcasted_iota(jnp.int32, (cols, LANE), 0)

        def part(ref):
            return ref[f, :, at].astype(F32)

        def column(edge, top, end):
            return jnp.concatenate([top, edge, end], axis=0)

        def corners(side):
            tiles = channels // LANE
            wide = -(-tiles // cols)
            first = channels + (side * wide + lax.rem(i, wide)) * LANE
            lanes = pl.ds(pl.multiple_of(first, LANE), LANE)
            both_lines = chosen(
                row_e[f, :, lanes].astype(F32), row_o[f, :, lanes].astype(F32), *in_rows
            )
            return [pltpu.roll(x, lax.rem(cols - i // wide, cols), 0)[:1] for x in both_lines]

        def taps(b):
            return [w[3 * a + b : 3 * a + b + 1] for a in range(3)]

        def along(taps, z):
            return sum(tap * z[a : a + rows] for a, tap in enumerate(taps))

        up, down = chosen(part(row_e), part(row_o), *in_rows)
        x = jnp.concatenate([up[None], hidden[f, :, :, at].astype(F32), down[None]], axis=0)
        total = along([tap[None] for tap in taps(1)], x) + bias[pl.ds(i, 1), :][None]
        for b, shift, edge in ((0, 1, 0), (2, cols - 1, cols - 1)):
            inside = [jnp.where(spot == edge, 0.0, tap)[None] for tap in taps(b)]
            total = total + along(inside, pltpu.roll(x, shift, 1))
        if n_cols == 2:
            sides = [jnp.where(col == 0, right, left) for left, right in zip(taps(0), taps(2))]
            beside = column(part(col_e), *corners(0))
            terms = [(jnp.where(col == 0, cols - 1, 0), along(sides, beside))]
        else:
            edges = chosen(part(col_e), part(col_o), col, n_cols)
            terms = [
                (border, along(taps(b), column(edge, *corners(side))))
                for side, (border, b, edge) in enumerate(zip((0, cols - 1), (0, 2), edges))
                if n_cols > 1
            ]
        for edge, term in terms:
            total = total + jnp.where((spot == edge)[None], term[:, None, :], 0.0)
        return total

    def tile(i, carry):
        first = pl.multiple_of(i * LANE, LANE)
        for f in range(frames):
            value, gate = conv(f, i), conv(f, i + steps)
            held[f, :, :, pl.ds(first, LANE)] = (
                0.5 * value * gate * (1.0 + jnp.tanh(0.5 * gate))
            ).astype(BF16)
        return carry

    stores = []
    for part in range(parts):
        lo, hi = steps * part // parts, steps * (part + 1) // parts
        lax.fori_loop(lo, hi, tile, 0)
        at = pl.ds(lo * LANE, (hi - lo) * LANE)
        for f in range(frames):
            stores.append(
                pltpu.make_async_copy(
                    held.at[f, :, :, at], out.at[f, :, :, at], sems.at[part, f]
                )
            )
            stores[-1].start()
    for copy in stores:
        copy.wait()


def swaps(n):
    even = [min(i ^ 1, n - 1) for i in range(n)]
    odd = [min(max(((i - 1) ^ 1) + 1, 0), n - 1) for i in range(n)]
    return [list(enumerate(to)) for to in ((even, odd) if n > 2 else (even,))]


def sends(first, last, axis):
    is_even = lax.rem(lax.axis_index(axis), 2) == 0
    return jnp.where(is_even, last, first), jnp.where(is_even, first, last)


def halo_sends(hidden):
    rows, cols = hidden.shape[1:3]
    to_rows = sends(hidden[:, 0], hidden[:, rows - 1], ROW)
    return to_rows, sends(hidden[:, :, 0], hidden[:, :, cols - 1], "col")


def with_corners(to_rows, by_cols):
    frames, cols, channels = to_rows[0].shape
    n_cols = lax.axis_size("col")
    if n_cols == 1:
        return to_rows
    sides = by_cols[:1] if n_cols == 2 else chosen(*by_cols, *place("col"))
    wide = -(-channels // (cols * LANE)) * LANE
    packed = []
    for side in sides:
        corners = sends(side[:, 0], side[:, side.shape[1] - 1], ROW)
        spare = ((0, 0), (0, cols * wide - channels))
        packed.append([jnp.pad(x, spare).reshape(frames, cols, wide) for x in corners])
    return [jnp.concatenate(parts, axis=2) for parts in zip(to_rows, *packed)]


def both(results):
    return [results[0], results[-1]]


def swap_even_rows(to_even):
    return lax.ppermute(to_even, ROW, swaps(lax.axis_size(ROW))[0])


def swap_odd_rows(to_odd):
    pairs = swaps(lax.axis_size(ROW))[1:]
    return lax.ppermute(to_odd, ROW, pairs[0]) if pairs else to_odd


def swap_columns(to_cols):
    pairs = swaps(lax.axis_size("col"))
    return both([lax.ppermute(x, "col", p) for x, p in zip(to_cols, pairs)])


def convolve(hidden, around, weight, bias):
    frames, rows, cols, channels = hidden.shape
    result = jax.ShapeDtypeStruct((frames, rows, cols, channels // 2), BF16)
    return pl.pallas_call(
        conv_kernel,
        out_shape=result,
        in_specs=whole(3 + len(around)),
        out_specs=pl.BlockSpec(memory_space=pl.ANY),
        scratch_shapes=[pltpu.VMEM(result.shape, BF16), pltpu.SemaphoreType.DMA((2, frames))],
        compiler_params=pltpu.CompilerParams(vmem_limit_bytes=VMEM_LIMIT),
        cost_estimate=pl.CostEstimate(
            flops=20 * hidden.size, bytes_accessed=4 * hidden.size, transcendentals=hidden.size // 2
        ),
        name="conv_gate",
    )(hidden, *around, weight, bias.reshape(-1, LANE))


ROW = ("row_far", "row_near")
GROUP = ("row_near", "col")


def across(value):
    n = lax.axis_size("row_far")
    return [
        lax.ppermute(value, "row_far", [(i, (i + step) % n) for i in range(n)])
        for step in range(1, n)
    ]


def exchange(value, step):
    n = lax.axis_size(GROUP)
    return lax.ppermute(value, GROUP, [(i, target(i, step, n)) for i in range(n)])


def frame_prefix(value):
    n, mine = lax.axis_size("frame"), lax.axis_index("frame")
    running = value
    doubling = n & (n - 1) == 0
    step = 1
    while step < n:
        pairs = [(i, i ^ step if doubling else (i + step) % n) for i in range(n)]
        got = lax.ppermute(value, "frame", pairs)
        running = running + jnp.where(mine & step != 0 if doubling else mine >= step, got, 0)
        value = value + got if doubling else value
        step = 2 * step if doubling else step + 1
    return running


def on_device(queries, keys, values, hidden, conv_weight, conv_bias):
    width = queries.shape[-1]
    tokens = queries.size // width
    pieces = lax.axis_size(GROUP)
    per = piece_rows(width, pieces)

    local = pl.pallas_call(
        functools.partial(state_kernel, width, pieces),
        out_shape=[jax.ShapeDtypeStruct((per // 8, 8, LANE), F32)] * pieces,
        in_specs=[pl.BlockSpec(memory_space=pltpu.HBM)] * 2,
        out_specs=whole(pieces),
        scratch_shapes=[
            pltpu.VMEM((tokens, width), BF16),
            pltpu.VMEM((tokens, width), BF16),
            pltpu.VMEM((pieces * per, LANE), F32),
            pltpu.SemaphoreType.DMA((2, 2)),
        ],
        compiler_params=pltpu.CompilerParams(vmem_limit_bytes=VMEM_MOST),
        cost_estimate=pl.CostEstimate(
            flops=2 * tokens * width * HD, bytes_accessed=6 * tokens * width, transcendentals=0
        ),
        name="local_state",
    )(keys.reshape(tokens, width), values.reshape(tokens, width))

    near = sum((exchange(local[step], step) for step in range(1, pieces)), local[0])
    near, (to_rows, to_cols) = lax.optimization_barrier((near, halo_sends(hidden)))
    block, by_cols, to_rows = lax.optimization_barrier(
        (sum(across(near), near), swap_columns(to_cols), to_rows)
    )

    prefix = frame_prefix(block)
    to_even, to_odd = with_corners(to_rows, by_cols)
    by_rows = swap_even_rows(to_even), swap_odd_rows(to_odd)
    quarters = [prefix, *(exchange(prefix, step) for step in range(1, pieces))]
    halos = (*by_rows, *by_cols)
    gated = convolve(hidden, halos, conv_weight, conv_bias)
    attended = pl.pallas_call(
        functools.partial(attend_kernel, width),
        out_shape=jax.ShapeDtypeStruct((tokens, width), BF16),
        in_specs=whole(1 + pieces),
        out_specs=pl.BlockSpec(memory_space=pl.ANY),
        scratch_shapes=[
            pltpu.VMEM((pieces * per, LANE), F32),
            pltpu.VMEM((tokens, width), BF16),
            pltpu.SemaphoreType.DMA((3,)),
        ],
        compiler_params=pltpu.CompilerParams(vmem_limit_bytes=VMEM_LIMIT),
        cost_estimate=pl.CostEstimate(
            flops=8 * tokens * width * HD, bytes_accessed=6 * tokens * width, transcendentals=0
        ),
        name="attend",
    )(queries.reshape(tokens, width), *quarters)
    return attended.reshape(queries.shape), gated


def solution(mesh):
    frame, row, col = (mesh.shape[name] for name in ("frame", "row", "col"))
    near = 2 if row % 2 == 0 else 1
    split = jax.sharding.Mesh(
        mesh.devices.reshape(frame, row // near, near, col), ("frame", *ROW, "col")
    )
    placed = P("frame", ROW, "col", None)
    return jax.shard_map(
        on_device,
        mesh=split,
        in_specs=(placed, placed, placed, placed, P(), P()),
        out_specs=(placed, placed),
        check_vma=False,
    )
```

time: 169 us -> 36.9 us (0.22)
  the two profiles are of different devices: /device:TPU:0 before, /device:TPU:16 now
where the time goes in v1:
time: 36.9 us; the launch traced here: 36.7 us
  starting transfers between devices  13.5 us (37%)
  waiting for transfers between devices  11 us (30%)
  Pallas kernels  8.62 us (23%)
  local copies, waits for them, and re-layouts  2.52 us (7%)
  between operations  0.84 us (2%)
    ppermute x6, starting transfers between devices, exchange(): lax.ppermute(value, GROUP, [(i, target(i, step, n)) for i in range(n)])  7.11 us
    ppermute x1, waiting for transfers between devices, across(): lax.ppermute(value, 'row_far', [(i, (i + step) % n) for i in range(n)])  5.06 us
    pallas_call x1, Pallas kernels, convolve(): pl.pallas_call(conv_kernel, out_shape=result, in_specs=whole(3 + len(arou...  4.5 us
    ppermute x6, waiting for transfers between devices, exchange(): lax.ppermute(value, GROUP, [(i, target(i, step, n)) for i in range(n)])  2.6 us
    pallas_call x1, Pallas kernels, on_device(): pl.pallas_call(functools.partial(state_kernel, width, pieces), out_shape=...  2.56 us
    slice x1, local copies, waits for them, and re-layouts, halo_sends(): return (to_rows, sends(hidden[:, :, 0], hidden[:, :, cols - 1], 'col'))  2.39 us
    ppermute x1, waiting for transfers between devices, swap_odd_rows(): return lax.ppermute(to_odd, ROW, pairs[0]) if pairs else to_odd  2.27 us
    ppermute x1, starting transfers between devices, swap_even_rows(): return lax.ppermute(to_even, ROW, swaps(lax.axis_size(ROW))[0])  1.94 us
  transfers between devices with their start and end apart: 12, of which 5 were waited for; matrix products, arithmetic and copies ran while one was open for 8% of the time, Pallas kernels for 12%

profile of v1, /device:TPU:16, one launch (start us, length us, event | category | flops | bytes accessed | tf_op | source)
XLA Modules:
  0.0 36.7 jit_solution(12576922763855498362)
XLA Ops:
  0.6 0.0 copy-start
  0.6 2.6 %local_state.1 = (f32[19,8,128]{2,1,0:T(8,128)}, f32[19,8,128]{2,1,0:T(8,128)}, f32[19,8,128]{2,1,0:T(8,128)}, f32[19,8,128]{2,1,0:T(8,128)}) custom-call(bf16[128,2240]{1,0:T(8,128)(2,1)} %bitcast.35, bf16[128,2240]{1,0:T(8,128)(2,1)} %bitcast.36), custom_call_target="tpu_custom_call" | custom-call | flops 18350080 | bytes 1720320 | tf_op jit(solution)/shard_map/local_state/pallas_call | solution.py:329
  3.2 1.6 %collective-permute-start = (f32[19,8,128]{2,1,0:T(8,128)}, f32[19,8,128]{2,1,0:T(8,128)S(1)}, u32[]{:S(2)}, u32[]{:S(2)}) collective-permute-start(f32[19,8,128]{2,1,0:T(8,128)} %get-tuple-element.16), channel_id=1, source_target_pairs={{0,1},{1,0},{2,3},{3,2},{4,5},{5,4},{6,7},{7,6},{8,9},{9,8},{10,11... | collective-permute-start | bytes 233480 | tf_op jit(solution)/shard_map/ppermute | solution.py:306
  4.8 1.6 %collective-permute-start.1 = (f32[19,8,128]{2,1,0:T(8,128)}, f32[19,8,128]{2,1,0:T(8,128)S(1)}, u32[]{:S(2)}, u32[]{:S(2)}) collective-permute-start(f32[19,8,128]{2,1,0:T(8,128)} %get-tuple-element.17), channel_id=1, source_target_pairs={{0,2},{1,3},{2,0},{3,1},{4,6},{5,7},{6,4},{7,5},{8,10},{9,11},{10,... | collective-permute-start | bytes 233480 | tf_op jit(solution)/shard_map/ppermute | solution.py:306
  6.4 0.4 %collective-permute-start.2 = (f32[19,8,128]{2,1,0:T(8,128)}, f32[19,8,128]{2,1,0:T(8,128)S(1)}, u32[]{:S(2)}, u32[]{:S(2)}) collective-permute-start(f32[19,8,128]{2,1,0:T(8,128)} %get-tuple-element.18), channel_id=1, source_target_pairs={{0,3},{1,2},{2,1},{3,0},{4,7},{5,6},{6,5},{7,4},{8,11},{9,10},{10,... | collective-permute-start | bytes 233480 | tf_op jit(solution)/shard_map/ppermute | solution.py:306
  6.8 0.0 copy-start.4
  6.8 2.4 %fusion.3 = (bf16[2,8,1,5632]{3,2,1,0:T(2,128)(2,1)S(1)}, bf16[2,8,1,5632]{3,2,1,0:T(2,128)(2,1)S(1)}) fusion(bf16[2,8,8,5632]{3,2,1,0:T(8,128)(2,1)} %hidden.1), kind=kLoop, calls=%fused_computation.16 | loop fusion | bytes 720896 | tf_op jit(solution)/shard_map/slice | solution.py:239
  9.2 0.0 copy-done
  9.2 0.1 fusion.2
  9.3 0.0 copy-start.2
  9.3 0.0 copy-start.3
  9.3 0.0 collective-permute-done
  9.3 0.8 %collective-permute-done.1 = f32[19,8,128]{2,1,0:T(8,128)S(1)} collective-permute-done((f32[19,8,128]{2,1,0:T(8,128)}, f32[19,8,128]{2,1,0:T(8,128)S(1)}, u32[]{:S(2)}, u32[]{:S(2)}) %collective-permute-start.1) | collective-permute-done | bytes 77856 | tf_op jit(solution)/shard_map/ppermute | solution.py:306
  10.1 1.8 %collective-permute-done.2 = f32[19,8,128]{2,1,0:T(8,128)S(1)} collective-permute-done((f32[19,8,128]{2,1,0:T(8,128)}, f32[19,8,128]{2,1,0:T(8,128)S(1)}, u32[]{:S(2)}, u32[]{:S(2)}) %collective-permute-start.2) | collective-permute-done | bytes 77856 | tf_op jit(solution)/shard_map/ppermute | solution.py:306
  11.9 0.0 copy-done.4
  11.9 0.6 %collective-permute-start.4 = (bf16[2,8,5632]{2,1,0:T(8,128)(2,1)S(1)}, bf16[2,8,5632]{2,1,0:T(8,128)(2,1)S(1)}, u32[]{:S(2)}, u32[]{:S(2)}) collective-permute-start(bf16[2,8,5632]{2,1,0:T(8,128)(2,1)S(1)} %fusion.2), channel_id=1, source_target_pairs={{0,1},{1,0},{2,3},{3,2},{4,5},{5,4},{6,7},{7,6},{8,9},{9,8},{10,11... | collective-permute-start | bytes 540680 | tf_op jit(solution)/shard_map/ppermute | solution.py:272
  12.5 0.3 collective-permute-start.3
  12.8 5.1 %collective-permute-done.3 = f32[19,8,128]{2,1,0:T(8,128)S(1)} collective-permute-done((f32[19,8,128]{2,1,0:T(8,128)S(1)}, f32[19,8,128]{2,1,0:T(8,128)S(1)}, u32[]{:S(2)}, u32[]{:S(2)}) %collective-permute-start.3) | collective-permute-done | bytes 77856 | tf_op jit(solution)/shard_map/ppermute | solution.py:299
  17.9 0.0 collective-permute-done.4.col_e.col_o
  17.9 0.1 collective-permute-start.5
  18.0 0.1 broadcast_select_fusion
  18.3 1.9 %collective-permute-start.10 = (bf16[2,8,6400]{2,1,0:T(8,128)(2,1)S(1)}, bf16[2,8,6400]{2,1,0:T(8,128)(2,1)S(1)}, u32[]{:S(2)}, u32[]{:S(2)}) collective-permute-start(bf16[2,8,6400]{2,1,0:T(8,128)(2,1)S(1)} %pad_maximum_fusion), channel_id=1, source_target_pairs={{0,2},{2,0},{4,6},{6,4},{1,3},{3,1},{5,7},{7,5},{8,10},{10,8},{12,... | collective-permute-start | bytes 614408 | tf_op jit(solution)/shard_map/ppermute | solution.py:262
  20.2 0.0 collective-permute-done.5
  20.2 1.6 %collective-permute-start.6 = (f32[19,8,128]{2,1,0:T(8,128)S(1)}, f32[19,8,128]{2,1,0:T(8,128)S(1)}, u32[]{:S(2)}, u32[]{:S(2)}) collective-permute-start(f32[19,8,128]{2,1,0:T(8,128)S(1)} %add.35), channel_id=1, source_target_pairs={{0,16},{8,24},{16,0},{24,8},{1,17},{9,25},{17,1},{25,9},{2,18},{10... | collective-permute-start | bytes 233480 | tf_op jit(solution)/shard_map/ppermute | solution.py:316
  21.8 1.9 %collective-permute-start.11 = (bf16[2,8,6400]{2,1,0:T(8,128)(2,1)S(1)}, bf16[2,8,6400]{2,1,0:T(8,128)(2,1)S(1)}, u32[]{:S(2)}, u32[]{:S(2)}) collective-permute-start(bf16[2,8,6400]{2,1,0:T(8,128)(2,1)S(1)} %pad_maximum_fusion.1), channel_id=1, source_target_pairs={{0,0},{2,4},{4,2},{6,6},{1,1},{3,5},{5,3},{7,7},{8,8},{10,12},{12,... | collective-permute-start | bytes 614408 | tf_op jit(solution)/shard_map/ppermute | solution.py:267
  23.7 1.0 %collective-permute-done.6 = f32[19,8,128]{2,1,0:T(8,128)S(1)} collective-permute-done((f32[19,8,128]{2,1,0:T(8,128)S(1)}, f32[19,8,128]{2,1,0:T(8,128)S(1)}, u32[]{:S(2)}, u32[]{:S(2)}) %collective-permute-start.6) | collective-permute-done | bytes 77856 | tf_op jit(solution)/shard_map/ppermute | solution.py:316
  24.8 1.1 %collective-permute-start.9 = (f32[19,8,128]{2,1,0:T(8,128)S(1)}, f32[19,8,128]{2,1,0:T(8,128)S(1)}, u32[]{:S(2)}, u32[]{:S(2)}) collective-permute-start(f32[19,8,128]{2,1,0:T(8,128)S(1)} %select_add_fusion.refs_0_), channel_id=1, source_target_pairs={{0,3},{1,2},{2,1},{3,0},{4,7},{5,6},{6,5},{7,4},{8,11},{9,10},{10,... | collective-permute-start | bytes 233480 | tf_op jit(solution)/shard_map/ppermute | solution.py:306
  25.9 0.8 %collective-permute-start.8 = (f32[19,8,128]{2,1,0:T(8,128)S(1)}, f32[19,8,128]{2,1,0:T(8,128)S(1)}, u32[]{:S(2)}, u32[]{:S(2)}) collective-permute-start(f32[19,8,128]{2,1,0:T(8,128)S(1)} %select_add_fusion.refs_0_), channel_id=1, source_target_pairs={{0,2},{1,3},{2,0},{3,1},{4,6},{5,7},{6,4},{7,5},{8,10},{9,11},{10,... | collective-permute-start | bytes 233480 | tf_op jit(solution)/shard_map/ppermute | solution.py:306
  26.7 1.6 %collective-permute-start.7 = (f32[19,8,128]{2,1,0:T(8,128)S(1)}, f32[19,8,128]{2,1,0:T(8,128)S(1)}, u32[]{:S(2)}, u32[]{:S(2)}) collective-permute-start(f32[19,8,128]{2,1,0:T(8,128)S(1)} %select_add_fusion.refs_0_), channel_id=1, source_target_pairs={{0,1},{1,0},{2,3},{3,2},{4,5},{5,4},{6,7},{7,6},{8,9},{9,8},{10,11... | collective-permute-start | bytes 233480 | tf_op jit(solution)/shard_map/ppermute | solution.py:306
  28.3 0.0 collective-permute-done.10.row_e
  28.3 2.3 %collective-permute-done.11.row_o = bf16[2,8,6400]{2,1,0:T(8,128)(2,1)S(1)} collective-permute-done((bf16[2,8,6400]{2,1,0:T(8,128)(2,1)S(1)}, bf16[2,8,6400]{2,1,0:T(8,128)(2,1)S(1)}, u32[]{:S(2)}, u32[]{:S(2)}) %collective-permute-start.11) | collective-permute-done | bytes 204832 | tf_op jit(solution)/shard_map/ppermute | solution.py:267
  30.6 0.0 copy-done.2
  30.6 0.0 copy-done.3
  30.6 0.0 copy-start.1
  30.6 4.5 %conv_gate.1 = bf16[2,8,8,2816]{3,2,1,0:T(8,128)(2,1)} custom-call(bf16[2,8,8,5632]{3,2,1,0:T(8,128)(2,1)S(1)} %copy-done, bf16[2,8,6400]{2,1,0:T(8,128)(2,1)S(1)} %collective-permute-done.10.row_e, bf16[2,8,6400]{2,1,0:T(8,128)(2,1)S(1)} %collective-permute-done.11.row_o, bf16[2,8,5632]{2,1,0:T(8,128)(2,1)S(1)} %collective-permute-done.4.col_e.col_o, ...), custom_call_target="tpu_custom_call" | custom-call | flops 14417920 | bytes 2883584 | tf_op jit(solution)/shard_map/conv_gate/pallas_call | solution.py:278
  35.1 0.0 collective-permute-done.9.refs_3_
  35.1 0.0 collective-permute-done.8.refs_2_
  35.1 0.0 collective-permute-done.7.refs_1_
  35.2 0.0 copy-done.1
  35.2 1.6 %attend.1 = bf16[128,2240]{1,0:T(8,128)(2,1)} custom-call(bf16[128,2240]{1,0:T(8,128)(2,1)S(1)} %bitcast.33, f32[19,8,128]{2,1,0:T(8,128)S(1)} %select_add_fusion.refs_0_, f32[19,8,128]{2,1,0:T(8,128)S(1)} %collective-permute-done.7.refs_1_, f32[19,8,128]{2,1,0:T(8,128)S(1)} %collective-permute-done.8.refs_2_, f32[19,8,128]{2,1,0:T(8,128)S(1)} %collective-permute-done.9.refs_3_), custom_call_target="tpu_custom_call" | custom-call | flops 73400320 | bytes 1720320 | tf_op jit(solution)/shard_map/attend/pallas_call | solution.py:359
  (12 shorter events, 0.2 us)
Async XLA Ops:
  0.6 8.5 %copy-start = (bf16[2,8,8,5632]{3,2,1,0:T(8,128)(2,1)S(1)}, bf16[2,8,8,5632]{3,2,1,0:T(8,128)(2,1)}, u32[]{:S(2)}) copy-start(bf16[2,8,8,5632]{3,2,1,0:T(8,128)(2,1)} %hidden.1) | copy-start | bytes 4325380
  3.2 6.1 %collective-permute-start = (f32[19,8,128]{2,1,0:T(8,128)}, f32[19,8,128]{2,1,0:T(8,128)S(1)}, u32[]{:S(2)}, u32[]{:S(2)}) collective-permute-start(f32[19,8,128]{2,1,0:T(8,128)} %get-tuple-element.16), channel_id=1, source_target_pairs={{0,1},{1,0},{2,3},{3,2},{4,5},{5,4},{6,7},{7,6},{8,9},{9,8},{10,11... | collective-permute-start | bytes 233480 | tf_op jit(solution)/shard_map/ppermute | solution.py:306
  4.8 5.3 %collective-permute-start.1 = (f32[19,8,128]{2,1,0:T(8,128)}, f32[19,8,128]{2,1,0:T(8,128)S(1)}, u32[]{:S(2)}, u32[]{:S(2)}) collective-permute-start(f32[19,8,128]{2,1,0:T(8,128)} %get-tuple-element.17), channel_id=1, source_target_pairs={{0,2},{1,3},{2,0},{3,1},{4,6},{5,7},{6,4},{7,5},{8,10},{9,11},{10,... | collective-permute-start | bytes 233480 | tf_op jit(solution)/shard_map/ppermute | solution.py:306
  6.4 5.5 %collective-permute-start.2 = (f32[19,8,128]{2,1,0:T(8,128)}, f32[19,8,128]{2,1,0:T(8,128)S(1)}, u32[]{:S(2)}, u32[]{:S(2)}) collective-permute-start(f32[19,8,128]{2,1,0:T(8,128)} %get-tuple-element.18), channel_id=1, source_target_pairs={{0,3},{1,2},{2,1},{3,0},{4,7},{5,6},{6,5},{7,4},{8,11},{9,10},{10,... | collective-permute-start | bytes 233480 | tf_op jit(solution)/shard_map/ppermute | solution.py:306
  6.8 5.1 %copy-start.4 = (f32[19,8,128]{2,1,0:T(8,128)S(1)}, f32[19,8,128]{2,1,0:T(8,128)}, u32[]{:S(2)}) copy-start(f32[19,8,128]{2,1,0:T(8,128)} %get-tuple-element.15) | copy-start | bytes 233476
  9.3 21.4 %copy-start.2 = (f32[9,5632]{1,0:T(8,128)S(1)}, f32[9,5632]{1,0:T(8,128)}, u32[]{:S(2)}) copy-start(f32[9,5632]{1,0:T(8,128)} %weight.1) | copy-start | bytes 608260
  9.3 21.3 %copy-start.3 = (f32[5632]{0:T(1024)S(1)}, f32[5632]{0:T(1024)}, u32[]{:S(2)}) copy-start(f32[5632]{0:T(1024)} %param.11) | copy-start | bytes 67588
  11.9 6.0 %collective-permute-start.4 = (bf16[2,8,5632]{2,1,0:T(8,128)(2,1)S(1)}, bf16[2,8,5632]{2,1,0:T(8,128)(2,1)S(1)}, u32[]{:S(2)}, u32[]{:S(2)}) collective-permute-start(bf16[2,8,5632]{2,1,0:T(8,128)(2,1)S(1)} %fusion.2), channel_id=1, source_target_pairs={{0,1},{1,0},{2,3},{3,2},{4,5},{5,4},{6,7},{7,6},{8,9},{9,8},{10,11... | collective-permute-start | bytes 540680 | tf_op jit(solution)/shard_map/ppermute | solution.py:272
  12.5 5.4 %collective-permute-start.3 = (f32[19,8,128]{2,1,0:T(8,128)S(1)}, f32[19,8,128]{2,1,0:T(8,128)S(1)}, u32[]{:S(2)}, u32[]{:S(2)}) collective-permute-start(f32[19,8,128]{2,1,0:T(8,128)S(1)} %add_add_fusion), channel_id=1, source_target_pairs={{0,4},{4,0},{1,5},{5,1},{2,6},{6,2},{3,7},{7,3},{8,12},{12,8},{9,1... | collective-permute-start | bytes 233480 | tf_op jit(solution)/shard_map/ppermute | solution.py:299
  17.9 2.3 %collective-permute-start.5 = (f32[19,8,128]{2,1,0:T(8,128)S(1)}, f32[19,8,128]{2,1,0:T(8,128)S(1)}, u32[]{:S(2)}, u32[]{:S(2)}) collective-permute-start(f32[19,8,128]{2,1,0:T(8,128)S(1)} %add.33), channel_id=1, source_target_pairs={{0,8},{8,0},{16,24},{24,16},{1,9},{9,1},{17,25},{25,17},{2,10},{10... | collective-permute-start | bytes 233480 | tf_op jit(solution)/shard_map/ppermute | solution.py:316
  18.3 10.1 %collective-permute-start.10 = (bf16[2,8,6400]{2,1,0:T(8,128)(2,1)S(1)}, bf16[2,8,6400]{2,1,0:T(8,128)(2,1)S(1)}, u32[]{:S(2)}, u32[]{:S(2)}) collective-permute-start(bf16[2,8,6400]{2,1,0:T(8,128)(2,1)S(1)} %pad_maximum_fusion), channel_id=1, source_target_pairs={{0,2},{2,0},{4,6},{6,4},{1,3},{3,1},{5,7},{7,5},{8,10},{10,8},{12,... | collective-permute-start | bytes 614408 | tf_op jit(solution)/shard_map/ppermute | solution.py:262
  20.2 4.5 %collective-permute-start.6 = (f32[19,8,128]{2,1,0:T(8,128)S(1)}, f32[19,8,128]{2,1,0:T(8,128)S(1)}, u32[]{:S(2)}, u32[]{:S(2)}) collective-permute-start(f32[19,8,128]{2,1,0:T(8,128)S(1)} %add.35), channel_id=1, source_target_pairs={{0,16},{8,24},{16,0},{24,8},{1,17},{9,25},{17,1},{25,9},{2,18},{10... | collective-permute-start | bytes 233480 | tf_op jit(solution)/shard_map/ppermute | solution.py:316
  21.8 8.8 %collective-permute-start.11 = (bf16[2,8,6400]{2,1,0:T(8,128)(2,1)S(1)}, bf16[2,8,6400]{2,1,0:T(8,128)(2,1)S(1)}, u32[]{:S(2)}, u32[]{:S(2)}) collective-permute-start(bf16[2,8,6400]{2,1,0:T(8,128)(2,1)S(1)} %pad_maximum_fusion.1), channel_id=1, source_target_pairs={{0,0},{2,4},{4,2},{6,6},{1,1},{3,5},{5,3},{7,7},{8,8},{10,12},{12,... | collective-permute-start | bytes 614408 | tf_op jit(solution)/shard_map/ppermute | solution.py:267
  24.8 10.3 %collective-permute-start.9 = (f32[19,8,128]{2,1,0:T(8,128)S(1)}, f32[19,8,128]{2,1,0:T(8,128)S(1)}, u32[]{:S(2)}, u32[]{:S(2)}) collective-permute-start(f32[19,8,128]{2,1,0:T(8,128)S(1)} %select_add_fusion.refs_0_), channel_id=1, source_target_pairs={{0,3},{1,2},{2,1},{3,0},{4,7},{5,6},{6,5},{7,4},{8,11},{9,10},{10,... | collective-permute-start | bytes 233480 | tf_op jit(solution)/shard_map/ppermute | solution.py:306
  25.9 9.3 %collective-permute-start.8 = (f32[19,8,128]{2,1,0:T(8,128)S(1)}, f32[19,8,128]{2,1,0:T(8,128)S(1)}, u32[]{:S(2)}, u32[]{:S(2)}) collective-permute-start(f32[19,8,128]{2,1,0:T(8,128)S(1)} %select_add_fusion.refs_0_), channel_id=1, source_target_pairs={{0,2},{1,3},{2,0},{3,1},{4,6},{5,7},{6,4},{7,5},{8,10},{9,11},{10,... | collective-permute-start | bytes 233480 | tf_op jit(solution)/shard_map/ppermute | solution.py:306
  26.7 8.4 %collective-permute-start.7 = (f32[19,8,128]{2,1,0:T(8,128)S(1)}, f32[19,8,128]{2,1,0:T(8,128)S(1)}, u32[]{:S(2)}, u32[]{:S(2)}) collective-permute-start(f32[19,8,128]{2,1,0:T(8,128)S(1)} %select_add_fusion.refs_0_), channel_id=1, source_target_pairs={{0,1},{1,0},{2,3},{3,2},{4,5},{5,4},{6,7},{7,6},{8,9},{9,8},{10,11... | collective-permute-start | bytes 233480 | tf_op jit(solution)/shard_map/ppermute | solution.py:306
  30.6 4.5 %copy-start.1 = (bf16[2,8,8,2240]{3,2,1,0:T(8,128)(2,1)S(1)}, bf16[2,8,8,2240]{3,2,1,0:T(8,128)(2,1)}, u32[]{:S(2)}) copy-start(bf16[2,8,8,2240]{3,2,1,0:T(8,128)(2,1)} %param.6) | copy-start | bytes 1720324

commit v2 on v1

--- a/solution.py
+++ b/solution.py
@@ -92,7 +92,7 @@
 def attend_kernel(width, q_ref, *refs):
     *quarters, out, p_ref, out_ref, sems = refs
     mine, pieces = lax.axis_index(GROUP), len(quarters)
-    for step, quarter in enumerate(quarters):
+    for step, quarter in enumerate(reversed(quarters)):
         rows = piece(source(mine, step, pieces), 8 * quarter.shape[0])
         p_ref[rows, :] = quarter[...].reshape(-1, LANE)
     tiles = lane_tiles(width)
@@ -143,72 +143,9 @@
     return jnp.where(mine == 0, 0, before), jnp.where(mine == n - 1, 0, after)
 
 
-def conv_kernel(hidden, row_e, row_o, col_e, col_o, weight, bias, out, held, sems):
-    frames, rows, cols, channels = hidden.shape
-    half = channels // 2
-    in_rows, (col, n_cols) = place(ROW), place("col")
-    steps, parts = half // LANE, sems.shape[0]
-
-    def conv(f, i):
-        at = pl.ds(pl.multiple_of(i * LANE, LANE), LANE)
-        w = weight[:, at]
-        spot = lax.broadcasted_iota(jnp.int32, (cols, LANE), 0)
-
-        def part(ref):
-            return ref[f, :, at].astype(F32)
-
-        def column(edge, top, end):
-            return jnp.concatenate([top, edge, end], axis=0)
-
-        def corners(side):
-            tiles = channels // LANE
-            wide = -(-tiles // cols)
-            first = channels + (side * wide + lax.rem(i, wide)) * LANE
-            lanes = pl.ds(pl.multiple_of(first, LANE), LANE)
-            both_lines = chosen(
-                row_e[f, :, lanes].astype(F32), row_o[f, :, lanes].astype(F32), *in_rows
-            )
-            return [pltpu.roll(x, lax.rem(cols - i // wide, cols), 0)[:1] for x in both_lines]
-
-        def taps(b):
-            return [w[3 * a + b : 3 * a + b + 1] for a in range(3)]
-
-        def along(taps, z):
-            return sum(tap * z[a : a + rows] for a, tap in enumerate(taps))
-
-        up, down = chosen(part(row_e), part(row_o), *in_rows)
-        x = jnp.concatenate([up[None], hidden[f, :, :, at].astype(F32), down[None]], axis=0)
-        total = along([tap[None] for tap in taps(1)], x) + bias[pl.ds(i, 1), :][None]
-        for b, shift, edge in ((0, 1, 0), (2, cols - 1, cols - 1)):
-            inside = [jnp.where(spot == edge, 0.0, tap)[None] for tap in taps(b)]
-            total = total + along(inside, pltpu.roll(x, shift, 1))
-        if n_cols == 2:
-            sides = [jnp.where(col == 0, right, left) for left, right in zip(taps(0), taps(2))]
-            beside = column(part(col_e), *corners(0))
-            terms = [(jnp.where(col == 0, cols - 1, 0), along(sides, beside))]
-        else:
-            edges = chosen(part(col_e), part(col_o), col, n_cols)
-            terms = [
-                (border, along(taps(b), column(edge, *corners(side))))
-                for side, (border, b, edge) in enumerate(zip((0, cols - 1), (0, 2), edges))
-                if n_cols > 1
-            ]
-        for edge, term in terms:
-            total = total + jnp.where((spot == edge)[None], term[:, None, :], 0.0)
-        return total
-
-    def tile(i, carry):
-        first = pl.multiple_of(i * LANE, LANE)
-        for f in range(frames):
-            value, gate = conv(f, i), conv(f, i + steps)
-            held[f, :, :, pl.ds(first, LANE)] = (
-                0.5 * value * gate * (1.0 + jnp.tanh(0.5 * gate))
-            ).astype(BF16)
-        return carry
-
+def stored(frames, ends, held, out, sems, tile):
     stores = []
-    for part in range(parts):
-        lo, hi = steps * part // parts, steps * (part + 1) // parts
+    for part, (lo, hi) in enumerate(zip(ends, ends[1:])):
         lax.fori_loop(lo, hi, tile, 0)
         at = pl.ds(lo * LANE, (hi - lo) * LANE)
         for f in range(frames):
@@ -220,6 +157,107 @@
             stores[-1].start()
     for copy in stores:
         copy.wait()
+
+
+def lane_tile(i):
+    return pl.ds(pl.multiple_of(i * LANE, LANE), LANE)
+
+
+def tap_rows(w, b):
+    return [w[3 * a + b : 3 * a + b + 1] for a in range(3)]
+
+
+def inside(tap, b, cols):
+    spot = lax.broadcasted_iota(jnp.int32, (cols, LANE), 0)
+    return tap if b == 1 else jnp.where(spot == (0 if b == 0 else cols - 1), 0.0, tap)
+
+
+def moved(x, b, cols):
+    return x if b == 1 else pltpu.roll(x, 1 if b == 0 else cols - 1, x.ndim - 2)
+
+
+def inner_kernel(hidden, weight, bias, out, held, sems):
+    frames, rows, cols, channels = hidden.shape
+    steps, parts = channels // LANE, sems.shape[0]
+
+    def tile(i, carry):
+        at = lane_tile(i)
+        w = weight[:, at]
+        taps = [[inside(tap, b, cols)[None] for tap in tap_rows(w, b)] for b in range(3)]
+        none = jnp.zeros((1, cols, LANE), F32)
+        for f in range(frames):
+            x = jnp.concatenate([none, hidden[f, :, :, at].astype(F32), none], axis=0)
+            total = bias[pl.ds(i, 1), :][None]
+            for b in range(3):
+                y = moved(x, b, cols)
+                total = total + sum(tap * y[a : a + rows] for a, tap in enumerate(taps[b]))
+            held[f, :, :, at] = total
+        return carry
+
+    stored(frames, [steps * p // parts for p in range(parts + 1)], held, out, sems, tile)
+
+
+def outer_kernel(inner, row_o, row_e, col_e, col_o, weight, out, held, sems):
+    frames, rows, cols, channels = inner.shape
+    half = channels // 2
+    in_rows, (col, n_cols) = place(ROW), place("col")
+    steps, parts = half // LANE, sems.shape[0]
+
+    def conv(f, i):
+        at = lane_tile(i)
+        w = weight[:, at]
+        spot = lax.broadcasted_iota(jnp.int32, (cols, LANE), 0)
+
+        def part(ref, at=at):
+            return ref[f, :, at].astype(F32)
+
+        def corners(side):
+            wide = -(-(channels // LANE) // cols)
+            first = channels + (side * wide + lax.rem(i, wide)) * LANE
+            lanes = pl.ds(pl.multiple_of(first, LANE), LANE)
+            lines = chosen(part(row_e, lanes), part(row_o, lanes), *in_rows)
+            return [pltpu.roll(x, lax.rem(cols - i // wide, cols), 0)[:1] for x in lines]
+
+        def beside(taps, edge, top, end):
+            z = jnp.concatenate([top, edge, end], axis=0)
+            return sum(tap * z[a : a + rows] for a, tap in enumerate(taps))
+
+        def line(x, a):
+            return sum(
+                inside(tap_rows(w, b)[a], b, cols) * moved(x, b, cols) for b in range(3)
+            )
+
+        up, down = chosen(part(row_e), part(row_o), *in_rows)
+        top, end = line(up, 0), line(down, 2)
+        if n_cols == 2:
+            taps = [jnp.where(col == 0, r, l) for l, r in zip(tap_rows(w, 0), tap_rows(w, 2))]
+            border = jnp.where(col == 0, cols - 1, 0)
+            terms = [(border, beside(taps, part(col_e), *corners(0)))]
+        else:
+            edges = chosen(part(col_e), part(col_o), col, n_cols)
+            terms = [
+                (border, beside(tap_rows(w, b), edge, *corners(side)))
+                for side, (border, b, edge) in enumerate(zip((0, cols - 1), (0, 2), edges))
+                if n_cols > 1
+            ]
+        total = []
+        for r in range(rows):
+            here = inner[f, r, :, at]
+            for border, term in terms:
+                here = here + jnp.where(spot == border, term[r : r + 1], 0.0)
+            here = here + top if r == 0 else here
+            total.append(here + end if r == rows - 1 else here)
+        return total
+
+    def tile(i, carry):
+        for f in range(frames):
+            for r, (value, gate) in enumerate(zip(conv(f, i), conv(f, i + steps))):
+                held[f, r, :, lane_tile(i)] = (
+                    0.5 * value * gate * (1.0 + jnp.tanh(0.5 * gate))
+                ).astype(BF16)
+        return carry
+
+    stored(frames, [steps * p // parts for p in range(parts + 1)], held, out, sems, tile)
 
 
 def swaps(n):
@@ -272,21 +310,22 @@
     return both([lax.ppermute(x, "col", p) for x, p in zip(to_cols, pairs)])
 
 
-def convolve(hidden, around, weight, bias):
-    frames, rows, cols, channels = hidden.shape
-    result = jax.ShapeDtypeStruct((frames, rows, cols, channels // 2), BF16)
+def convolve(kernel, name, result, *arrays):
     return pl.pallas_call(
-        conv_kernel,
+        kernel,
         out_shape=result,
-        in_specs=whole(3 + len(around)),
+        in_specs=whole(len(arrays)),
         out_specs=pl.BlockSpec(memory_space=pl.ANY),
-        scratch_shapes=[pltpu.VMEM(result.shape, BF16), pltpu.SemaphoreType.DMA((2, frames))],
+        scratch_shapes=[
+            pltpu.VMEM(result.shape, result.dtype),
+            pltpu.SemaphoreType.DMA((2, result.shape[0])),
+        ],
         compiler_params=pltpu.CompilerParams(vmem_limit_bytes=VMEM_LIMIT),
         cost_estimate=pl.CostEstimate(
-            flops=20 * hidden.size, bytes_accessed=4 * hidden.size, transcendentals=hidden.size // 2
+            flops=20 * result.size, bytes_accessed=6 * result.size, transcendentals=0
         ),
-        name="conv_gate",
-    )(hidden, *around, weight, bias.reshape(-1, LANE))
+        name=name,
+    )(*arrays)
 
 
 ROW = ("row_far", "row_near")
@@ -345,17 +384,25 @@
     )(keys.reshape(tokens, width), values.reshape(tokens, width))
 
     near = sum((exchange(local[step], step) for step in range(1, pieces)), local[0])
-    near, (to_rows, to_cols) = lax.optimization_barrier((near, halo_sends(hidden)))
-    block, by_cols, to_rows = lax.optimization_barrier(
-        (sum(across(near), near), swap_columns(to_cols), to_rows)
+    near, (to_rows, to_cols), bias = lax.optimization_barrier(
+        (near, halo_sends(hidden), conv_bias)
     )
-
+    summed = jax.ShapeDtypeStruct(hidden.shape, F32)
+    inner = convolve(
+        inner_kernel, "conv_inner", summed, hidden, conv_weight, bias.reshape(-1, LANE)
+    )
+    block, by_cols, to_rows, inner = lax.optimization_barrier(
+        (sum(across(near), near), swap_columns(to_cols), to_rows, inner)
+    )
+
+    to_even, to_odd = with_corners(to_rows, by_cols)
     prefix = frame_prefix(block)
-    to_even, to_odd = with_corners(to_rows, by_cols)
     by_rows = swap_even_rows(to_even), swap_odd_rows(to_odd)
-    quarters = [prefix, *(exchange(prefix, step) for step in range(1, pieces))]
-    halos = (*by_rows, *by_cols)
-    gated = convolve(hidden, halos, conv_weight, conv_bias)
+    others = [exchange(prefix, step) for step in range(pieces - 1, 0, -1)]
+    halos = (*by_rows[::-1], *by_cols)
+    result = jax.ShapeDtypeStruct((*hidden.shape[:3], hidden.shape[3] // 2), BF16)
+    gated = convolve(outer_kernel, "conv_gate", result, inner, *halos, conv_weight)
+    others, gated = lax.optimization_barrier((others, gated))
     attended = pl.pallas_call(
         functools.partial(attend_kernel, width),
         out_shape=jax.ShapeDtypeStruct((tokens, width), BF16),
@@ -371,7 +418,7 @@
             flops=8 * tokens * width * HD, bytes_accessed=6 * tokens * width, transcendentals=0
         ),
         name="attend",
-    )(queries.reshape(tokens, width), *quarters)
+    )(queries.reshape(tokens, width), *others, prefix)
     return attended.reshape(queries.shape), gated
 
 

time: 36.9 us -> 35.2 us (0.954)
  the two profiles are of different devices: /device:TPU:16 before, /device:TPU:0 now
where the time goes in v2:
time: 35.2 us; the launch traced here: 35 us
  starting transfers between devices  14.3 us (41%)
  Pallas kernels  9.01 us (26%)
  waiting for transfers between devices  8.11 us (23%)
  local copies, waits for them, and re-layouts  2.54 us (7%)
  between operations  0.82 us (2%)
    ppermute x6, starting transfers between devices, exchange(): lax.ppermute(value, GROUP, [(i, target(i, step, n)) for i in range(n)])  8.36 us
    pallas_call x2, Pallas kernels, convolve(): pl.pallas_call(kernel, out_shape=result, in_specs=whole(len(arrays)), out...  4.89 us
    ppermute x6, waiting for transfers between devices, exchange(): lax.ppermute(value, GROUP, [(i, target(i, step, n)) for i in range(n)])  4.25 us
    ppermute x2, waiting for transfers between devices, frame_prefix(): got = lax.ppermute(value, 'frame', pairs)  2.94 us
    ppermute x1, starting transfers between devices, across(): lax.ppermute(value, 'row_far', [(i, (i + step) % n) for i in range(n)])  2.59 us
    pallas_call x1, Pallas kernels, on_device(): pl.pallas_call(functools.partial(state_kernel, width, pieces), out_shape=...  2.56 us
    slice x1, local copies, waits for them, and re-layouts, halo_sends(): return (to_rows, sends(hidden[:, :, 0], hidden[:, :, cols - 1], 'col'))  2.41 us
    ppermute x2, starting transfers between devices, frame_prefix(): got = lax.ppermute(value, 'frame', pairs)  1.63 us
  transfers between devices with their start and end apart: 12, of which 7 were waited for; matrix products, arithmetic and copies ran while one was open for 7% of the time, Pallas kernels for 14%

profile of v2, /device:TPU:0, one launch (start us, length us, event | category | flops | bytes accessed | tf_op | source)
XLA Modules:
  0.0 35.0 jit_solution(13922608358015182295)
XLA Ops:
  0.6 0.0 copy-start
  0.6 2.6 %local_state.1 = (f32[19,8,128]{2,1,0:T(8,128)}, f32[19,8,128]{2,1,0:T(8,128)}, f32[19,8,128]{2,1,0:T(8,128)}, f32[19,8,128]{2,1,0:T(8,128)}) custom-call(bf16[128,2240]{1,0:T(8,128)(2,1)} %bitcast.35, bf16[128,2240]{1,0:T(8,128)(2,1)} %bitcast.36), custom_call_target="tpu_custom_call" | custom-call | flops 18350080 | bytes 1720320 | tf_op jit(solution)/shard_map/local_state/pallas_call | solution.py:368
  3.2 3.0 %collective-permute-start = (f32[19,8,128]{2,1,0:T(8,128)}, f32[19,8,128]{2,1,0:T(8,128)S(1)}, u32[]{:S(2)}, u32[]{:S(2)}) collective-permute-start(f32[19,8,128]{2,1,0:T(8,128)} %get-tuple-element.22), channel_id=1, source_target_pairs={{0,1},{1,0},{2,3},{3,2},{4,5},{5,4},{6,7},{7,6},{8,9},{9,8},{10,11... | collective-permute-start | bytes 233480 | tf_op jit(solution)/shard_map/ppermute | solution.py:345
  6.2 1.6 %collective-permute-start.1 = (f32[19,8,128]{2,1,0:T(8,128)}, f32[19,8,128]{2,1,0:T(8,128)S(1)}, u32[]{:S(2)}, u32[]{:S(2)}) collective-permute-start(f32[19,8,128]{2,1,0:T(8,128)} %get-tuple-element.23), channel_id=1, source_target_pairs={{0,2},{1,3},{2,0},{3,1},{4,6},{5,7},{6,4},{7,5},{8,10},{9,11},{10,... | collective-permute-start | bytes 233480 | tf_op jit(solution)/shard_map/ppermute | solution.py:345
  7.8 0.0 collective-permute-start.2
  7.8 0.0 copy-start.4
  7.8 0.0 copy-start.1
  7.8 0.0 copy-start.3
  7.8 2.4 %fusion.3 = (bf16[2,8,1,5632]{3,2,1,0:T(2,128)(2,1)S(1)}, bf16[2,8,1,5632]{3,2,1,0:T(2,128)(2,1)S(1)}) fusion(bf16[2,8,8,5632]{3,2,1,0:T(8,128)(2,1)} %hidden.1), kind=kLoop, calls=%fused_computation.16 | loop fusion | bytes 720896 | tf_op jit(solution)/shard_map/slice | solution.py:277
  10.3 0.0 copy-done
  10.4 0.0 collective-permute-done
  10.4 1.1 %collective-permute-done.1 = f32[19,8,128]{2,1,0:T(8,128)S(1)} collective-permute-done((f32[19,8,128]{2,1,0:T(8,128)}, f32[19,8,128]{2,1,0:T(8,128)S(1)}, u32[]{:S(2)}, u32[]{:S(2)}) %collective-permute-start.1) | collective-permute-done | bytes 77856 | tf_op jit(solution)/shard_map/ppermute | solution.py:345
  11.5 1.8 %collective-permute-done.2 = f32[19,8,128]{2,1,0:T(8,128)S(1)} collective-permute-done((f32[19,8,128]{2,1,0:T(8,128)}, f32[19,8,128]{2,1,0:T(8,128)S(1)}, u32[]{:S(2)}, u32[]{:S(2)}) %collective-permute-start.2) | collective-permute-done | bytes 77856 | tf_op jit(solution)/shard_map/ppermute | solution.py:345
  13.3 0.0 copy-done.4
  13.4 0.6 %collective-permute-start.4 = (bf16[2,8,5632]{2,1,0:T(8,128)(2,1)S(1)}, bf16[2,8,5632]{2,1,0:T(8,128)(2,1)S(1)}, u32[]{:S(2)}, u32[]{:S(2)}) collective-permute-start(bf16[2,8,5632]{2,1,0:T(8,128)(2,1)S(1)} %fusion.2), channel_id=1, source_target_pairs={{0,1},{1,0},{2,3},{3,2},{4,5},{5,4},{6,7},{7,6},{8,9},{9,8},{10,11... | collective-permute-start | bytes 540680 | tf_op jit(solution)/shard_map/ppermute | solution.py:310
  13.9 2.6 %collective-permute-start.3 = (f32[19,8,128]{2,1,0:T(8,128)S(1)}, f32[19,8,128]{2,1,0:T(8,128)S(1)}, u32[]{:S(2)}, u32[]{:S(2)}) collective-permute-start(f32[19,8,128]{2,1,0:T(8,128)S(1)} %add_add_fusion), channel_id=1, source_target_pairs={{0,4},{4,0},{1,5},{5,1},{2,6},{6,2},{3,7},{7,3},{8,12},{12,8},{9,1... | collective-permute-start | bytes 233480 | tf_op jit(solution)/shard_map/ppermute | solution.py:338
  16.5 0.0 copy-done.1
  16.5 0.0 copy-done.3
  16.5 2.6 %conv_inner.1.inner = f32[2,8,8,5632]{3,2,1,0:T(8,128)S(1)} custom-call(bf16[2,8,8,5632]{3,2,1,0:T(8,128)(2,1)S(1)} %copy-done, f32[9,5632]{1,0:T(8,128)S(1)} %copy-done.1, f32[44,128]{1,0:T(8,128)S(1)} %bitcast.34), custom_call_target="tpu_custom_call" | custom-call | flops 14417920 | bytes 4325376 | tf_op jit(solution)/shard_map/conv_inner/pallas_call | solution.py:314
  19.1 0.9 %collective-permute-done.3 = f32[19,8,128]{2,1,0:T(8,128)S(1)} collective-permute-done((f32[19,8,128]{2,1,0:T(8,128)S(1)}, f32[19,8,128]{2,1,0:T(8,128)S(1)}, u32[]{:S(2)}, u32[]{:S(2)}) %collective-permute-start.3) | collective-permute-done | bytes 77856 | tf_op jit(solution)/shard_map/ppermute | solution.py:338
  20.1 0.0 collective-permute-done.4.col_e.col_o
  20.1 0.1 broadcast_select_fusion
  20.3 0.1 collective-permute-start.5
  20.4 0.5 %collective-permute-start.11 = (bf16[2,8,6400]{2,1,0:T(8,128)(2,1)S(1)}, bf16[2,8,6400]{2,1,0:T(8,128)(2,1)S(1)}, u32[]{:S(2)}, u32[]{:S(2)}) collective-permute-start(bf16[2,8,6400]{2,1,0:T(8,128)(2,1)S(1)} %pad_maximum_fusion.1), channel_id=1, source_target_pairs={{0,2},{2,0},{4,6},{6,4},{1,3},{3,1},{5,7},{7,5},{8,10},{10,8},{12,... | collective-permute-start | bytes 614408 | tf_op jit(solution)/shard_map/ppermute | solution.py:300
  20.9 0.7 %collective-permute-done.5 = f32[19,8,128]{2,1,0:T(8,128)S(1)} collective-permute-done((f32[19,8,128]{2,1,0:T(8,128)S(1)}, f32[19,8,128]{2,1,0:T(8,128)S(1)}, u32[]{:S(2)}, u32[]{:S(2)}) %collective-permute-start.5) | collective-permute-done | bytes 77856 | tf_op jit(solution)/shard_map/ppermute | solution.py:355
  21.6 1.6 %collective-permute-start.6 = (f32[19,8,128]{2,1,0:T(8,128)S(1)}, f32[19,8,128]{2,1,0:T(8,128)S(1)}, u32[]{:S(2)}, u32[]{:S(2)}) collective-permute-start(f32[19,8,128]{2,1,0:T(8,128)S(1)} %add.35), channel_id=1, source_target_pairs={{0,16},{8,24},{16,0},{24,8},{1,17},{9,25},{17,1},{25,9},{2,18},{10... | collective-permute-start | bytes 233480 | tf_op jit(solution)/shard_map/ppermute | solution.py:355
  23.2 0.7 %collective-permute-start.10 = (bf16[2,8,6400]{2,1,0:T(8,128)(2,1)S(1)}, bf16[2,8,6400]{2,1,0:T(8,128)(2,1)S(1)}, u32[]{:S(2)}, u32[]{:S(2)}) collective-permute-start(bf16[2,8,6400]{2,1,0:T(8,128)(2,1)S(1)} %pad_maximum_fusion), channel_id=1, source_target_pairs={{0,0},{2,4},{4,2},{6,6},{1,1},{3,5},{5,3},{7,7},{8,8},{10,12},{12,... | collective-permute-start | bytes 614408 | tf_op jit(solution)/shard_map/ppermute | solution.py:305
  23.9 2.2 %collective-permute-done.6 = f32[19,8,128]{2,1,0:T(8,128)S(1)} collective-permute-done((f32[19,8,128]{2,1,0:T(8,128)S(1)}, f32[19,8,128]{2,1,0:T(8,128)S(1)}, u32[]{:S(2)}, u32[]{:S(2)}) %collective-permute-start.6) | collective-permute-done | bytes 77856 | tf_op jit(solution)/shard_map/ppermute | solution.py:355
  26.1 0.0 copy-start.2
  26.2 2.4 %collective-permute-start.7 = (f32[19,8,128]{2,1,0:T(8,128)S(1)}, f32[19,8,128]{2,1,0:T(8,128)S(1)}, u32[]{:S(2)}, u32[]{:S(2)}) collective-permute-start(f32[19,8,128]{2,1,0:T(8,128)S(1)} %select_add_fusion.refs_3_), channel_id=1, source_target_pairs={{0,3},{1,2},{2,1},{3,0},{4,7},{5,6},{6,5},{7,4},{8,11},{9,10},{10,... | collective-permute-start | bytes 233480 | tf_op jit(solution)/shard_map/ppermute | solution.py:345
  28.5 0.6 %collective-permute-start.8 = (f32[19,8,128]{2,1,0:T(8,128)S(1)}, f32[19,8,128]{2,1,0:T(8,128)S(1)}, u32[]{:S(2)}, u32[]{:S(2)}) collective-permute-start(f32[19,8,128]{2,1,0:T(8,128)S(1)} %select_add_fusion.refs_3_), channel_id=1, source_target_pairs={{0,2},{1,3},{2,0},{3,1},{4,6},{5,7},{6,4},{7,5},{8,10},{9,11},{10,... | collective-permute-start | bytes 233480 | tf_op jit(solution)/shard_map/ppermute | solution.py:345
  29.1 0.8 %collective-permute-start.9 = (f32[19,8,128]{2,1,0:T(8,128)S(1)}, f32[19,8,128]{2,1,0:T(8,128)S(1)}, u32[]{:S(2)}, u32[]{:S(2)}) collective-permute-start(f32[19,8,128]{2,1,0:T(8,128)S(1)} %select_add_fusion.refs_3_), channel_id=1, source_target_pairs={{0,1},{1,0},{2,3},{3,2},{4,5},{5,4},{6,7},{7,6},{8,9},{9,8},{10,11... | collective-permute-start | bytes 233480 | tf_op jit(solution)/shard_map/ppermute | solution.py:345
  29.9 0.0 collective-permute-done.11.row_e
  29.9 0.0 collective-permute-done.10.row_o
  29.9 2.3 %conv_gate.1 = bf16[2,8,8,2816]{3,2,1,0:T(8,128)(2,1)} custom-call(f32[2,8,8,5632]{3,2,1,0:T(8,128)S(1)} %conv_inner.1.inner, bf16[2,8,6400]{2,1,0:T(8,128)(2,1)S(1)} %collective-permute-done.10.row_o, bf16[2,8,6400]{2,1,0:T(8,128)(2,1)S(1)} %collective-permute-done.11.row_e, bf16[2,8,5632]{2,1,0:T(8,128)(2,1)S(1)} %collective-permute-done.4.col_e.col_o, ...), custom_call_target="tpu_custom_call" | custom-call | flops 7208960 | bytes 2162688 | tf_op jit(solution)/shard_map/conv_gate/pallas_call | solution.py:314
  32.2 0.0 collective-permute-done.7.refs_0_
  32.2 0.7 %collective-permute-done.8.refs_1_ = f32[19,8,128]{2,1,0:T(8,128)S(1)} collective-permute-done((f32[19,8,128]{2,1,0:T(8,128)S(1)}, f32[19,8,128]{2,1,0:T(8,128)S(1)}, u32[]{:S(2)}, u32[]{:S(2)}) %collective-permute-start.8) | collective-permute-done | bytes 77856 | tf_op jit(solution)/shard_map/ppermute | solution.py:345
  32.9 0.5 %collective-permute-done.9.refs_2_ = f32[19,8,128]{2,1,0:T(8,128)S(1)} collective-permute-done((f32[19,8,128]{2,1,0:T(8,128)S(1)}, f32[19,8,128]{2,1,0:T(8,128)S(1)}, u32[]{:S(2)}, u32[]{:S(2)}) %collective-permute-start.9) | collective-permute-done | bytes 77856 | tf_op jit(solution)/shard_map/ppermute | solution.py:345
  33.5 0.0 copy-done.2
  33.5 1.6 %attend.1 = bf16[128,2240]{1,0:T(8,128)(2,1)} custom-call(bf16[128,2240]{1,0:T(8,128)(2,1)S(1)} %bitcast.33, f32[19,8,128]{2,1,0:T(8,128)S(1)} %collective-permute-done.7.refs_0_, f32[19,8,128]{2,1,0:T(8,128)S(1)} %collective-permute-done.8.refs_1_, f32[19,8,128]{2,1,0:T(8,128)S(1)} %collective-permute-done.9.refs_2_, f32[19,8,128]{2,1,0:T(8,128)S(1)} %select_add_fusion.refs_3_), custom_call_target="tpu_custom_call" | custom-call | flops 73400320 | bytes 1720320 | tf_op jit(solution)/shard_map/attend/pallas_call | solution.py:406
  (13 shorter events, 0.3 us)
Async XLA Ops:
  0.6 9.6 %copy-start = (bf16[2,8,8,5632]{3,2,1,0:T(8,128)(2,1)S(1)}, bf16[2,8,8,5632]{3,2,1,0:T(8,128)(2,1)}, u32[]{:S(2)}) copy-start(bf16[2,8,8,5632]{3,2,1,0:T(8,128)(2,1)} %hidden.1) | copy-start | bytes 4325380
  3.2 7.2 %collective-permute-start = (f32[19,8,128]{2,1,0:T(8,128)}, f32[19,8,128]{2,1,0:T(8,128)S(1)}, u32[]{:S(2)}, u32[]{:S(2)}) collective-permute-start(f32[19,8,128]{2,1,0:T(8,128)} %get-tuple-element.22), channel_id=1, source_target_pairs={{0,1},{1,0},{2,3},{3,2},{4,5},{5,4},{6,7},{7,6},{8,9},{9,8},{10,11... | collective-permute-start | bytes 233480 | tf_op jit(solution)/shard_map/ppermute | solution.py:345
  6.2 5.3 %collective-permute-start.1 = (f32[19,8,128]{2,1,0:T(8,128)}, f32[19,8,128]{2,1,0:T(8,128)S(1)}, u32[]{:S(2)}, u32[]{:S(2)}) collective-permute-start(f32[19,8,128]{2,1,0:T(8,128)} %get-tuple-element.23), channel_id=1, source_target_pairs={{0,2},{1,3},{2,0},{3,1},{4,6},{5,7},{6,4},{7,5},{8,10},{9,11},{10,... | collective-permute-start | bytes 233480 | tf_op jit(solution)/shard_map/ppermute | solution.py:345
  7.8 5.5 %collective-permute-start.2 = (f32[19,8,128]{2,1,0:T(8,128)}, f32[19,8,128]{2,1,0:T(8,128)S(1)}, u32[]{:S(2)}, u32[]{:S(2)}) collective-permute-start(f32[19,8,128]{2,1,0:T(8,128)} %get-tuple-element.24), channel_id=1, source_target_pairs={{0,3},{1,2},{2,1},{3,0},{4,7},{5,6},{6,5},{7,4},{8,11},{9,10},{10,... | collective-permute-start | bytes 233480 | tf_op jit(solution)/shard_map/ppermute | solution.py:345
  7.8 5.5 %copy-start.4 = (f32[19,8,128]{2,1,0:T(8,128)S(1)}, f32[19,8,128]{2,1,0:T(8,128)}, u32[]{:S(2)}) copy-start(f32[19,8,128]{2,1,0:T(8,128)} %get-tuple-element.21) | copy-start | bytes 233476
  7.8 8.7 %copy-start.1 = (f32[9,5632]{1,0:T(8,128)S(1)}, f32[9,5632]{1,0:T(8,128)}, u32[]{:S(2)}) copy-start(f32[9,5632]{1,0:T(8,128)} %weight.3) | copy-start | bytes 608260
  7.8 8.7 %copy-start.3 = (f32[5632]{0:T(1024)S(1)}, f32[5632]{0:T(1024)}, u32[]{:S(2)}) copy-start(f32[5632]{0:T(1024)} %param.11) | copy-start | bytes 67588
  13.4 6.7 %collective-permute-start.4 = (bf16[2,8,5632]{2,1,0:T(8,128)(2,1)S(1)}, bf16[2,8,5632]{2,1,0:T(8,128)(2,1)S(1)}, u32[]{:S(2)}, u32[]{:S(2)}) collective-permute-start(bf16[2,8,5632]{2,1,0:T(8,128)(2,1)S(1)} %fusion.2), channel_id=1, source_target_pairs={{0,1},{1,0},{2,3},{3,2},{4,5},{5,4},{6,7},{7,6},{8,9},{9,8},{10,11... | collective-permute-start | bytes 540680 | tf_op jit(solution)/shard_map/ppermute | solution.py:310
  13.9 6.1 %collective-permute-start.3 = (f32[19,8,128]{2,1,0:T(8,128)S(1)}, f32[19,8,128]{2,1,0:T(8,128)S(1)}, u32[]{:S(2)}, u32[]{:S(2)}) collective-permute-start(f32[19,8,128]{2,1,0:T(8,128)S(1)} %add_add_fusion), channel_id=1, source_target_pairs={{0,4},{4,0},{1,5},{5,1},{2,6},{6,2},{3,7},{7,3},{8,12},{12,8},{9,1... | collective-permute-start | bytes 233480 | tf_op jit(solution)/shard_map/ppermute | solution.py:338
  20.3 1.3 %collective-permute-start.5 = (f32[19,8,128]{2,1,0:T(8,128)S(1)}, f32[19,8,128]{2,1,0:T(8,128)S(1)}, u32[]{:S(2)}, u32[]{:S(2)}) collective-permute-start(f32[19,8,128]{2,1,0:T(8,128)S(1)} %add.33), channel_id=1, source_target_pairs={{0,8},{8,0},{16,24},{24,16},{1,9},{9,1},{17,25},{25,17},{2,10},{10... | collective-permute-start | bytes 233480 | tf_op jit(solution)/shard_map/ppermute | solution.py:355
  20.4 9.5 %collective-permute-start.11 = (bf16[2,8,6400]{2,1,0:T(8,128)(2,1)S(1)}, bf16[2,8,6400]{2,1,0:T(8,128)(2,1)S(1)}, u32[]{:S(2)}, u32[]{:S(2)}) collective-permute-start(bf16[2,8,6400]{2,1,0:T(8,128)(2,1)S(1)} %pad_maximum_fusion.1), channel_id=1, source_target_pairs={{0,2},{2,0},{4,6},{6,4},{1,3},{3,1},{5,7},{7,5},{8,10},{10,8},{12,... | collective-permute-start | bytes 614408 | tf_op jit(solution)/shard_map/ppermute | solution.py:300
  21.6 4.5 %collective-permute-start.6 = (f32[19,8,128]{2,1,0:T(8,128)S(1)}, f32[19,8,128]{2,1,0:T(8,128)S(1)}, u32[]{:S(2)}, u32[]{:S(2)}) collective-permute-start(f32[19,8,128]{2,1,0:T(8,128)S(1)} %add.35), channel_id=1, source_target_pairs={{0,16},{8,24},{16,0},{24,8},{1,17},{9,25},{17,1},{25,9},{2,18},{10... | collective-permute-start | bytes 233480 | tf_op jit(solution)/shard_map/ppermute | solution.py:355
  23.2 6.7 %collective-permute-start.10 = (bf16[2,8,6400]{2,1,0:T(8,128)(2,1)S(1)}, bf16[2,8,6400]{2,1,0:T(8,128)(2,1)S(1)}, u32[]{:S(2)}, u32[]{:S(2)}) collective-permute-start(bf16[2,8,6400]{2,1,0:T(8,128)(2,1)S(1)} %pad_maximum_fusion), channel_id=1, source_target_pairs={{0,0},{2,4},{4,2},{6,6},{1,1},{3,5},{5,3},{7,7},{8,8},{10,12},{12,... | collective-permute-start | bytes 614408 | tf_op jit(solution)/shard_map/ppermute | solution.py:305
  26.1 7.3 %copy-start.2 = (bf16[2,8,8,2240]{3,2,1,0:T(8,128)(2,1)S(1)}, bf16[2,8,8,2240]{3,2,1,0:T(8,128)(2,1)}, u32[]{:S(2)}) copy-start(bf16[2,8,8,2240]{3,2,1,0:T(8,128)(2,1)} %param.6) | copy-start | bytes 1720324
  26.2 6.0 %collective-permute-start.7 = (f32[19,8,128]{2,1,0:T(8,128)S(1)}, f32[19,8,128]{2,1,0:T(8,128)S(1)}, u32[]{:S(2)}, u32[]{:S(2)}) collective-permute-start(f32[19,8,128]{2,1,0:T(8,128)S(1)} %select_add_fusion.refs_3_), channel_id=1, source_target_pairs={{0,3},{1,2},{2,1},{3,0},{4,7},{5,6},{6,5},{7,4},{8,11},{9,10},{10,... | collective-permute-start | bytes 233480 | tf_op jit(solution)/shard_map/ppermute | solution.py:345
  28.5 4.4 %collective-permute-start.8 = (f32[19,8,128]{2,1,0:T(8,128)S(1)}, f32[19,8,128]{2,1,0:T(8,128)S(1)}, u32[]{:S(2)}, u32[]{:S(2)}) collective-permute-start(f32[19,8,128]{2,1,0:T(8,128)S(1)} %select_add_fusion.refs_3_), channel_id=1, source_target_pairs={{0,2},{1,3},{2,0},{3,1},{4,6},{5,7},{6,4},{7,5},{8,10},{9,11},{10,... | collective-permute-start | bytes 233480 | tf_op jit(solution)/shard_map/ppermute | solution.py:345
  29.1 4.4 %collective-permute-start.9 = (f32[19,8,128]{2,1,0:T(8,128)S(1)}, f32[19,8,128]{2,1,0:T(8,128)S(1)}, u32[]{:S(2)}, u32[]{:S(2)}) collective-permute-start(f32[19,8,128]{2,1,0:T(8,128)S(1)} %select_add_fusion.refs_3_), channel_id=1, source_target_pairs={{0,1},{1,0},{2,3},{3,2},{4,5},{5,4},{6,7},{7,6},{8,9},{9,8},{10,11... | collective-permute-start | bytes 233480 | tf_op jit(solution)/shard_map/ppermute | solution.py:345

commit v3 on v2

--- a/solution.py
+++ b/solution.py
@@ -48,7 +48,7 @@
 
 
 def state_kernel(width, pieces, keys, values, *refs):
-    *outs, k_ref, v_ref, held, sems = refs
+    *outs, k_ref, v_ref, held, sems, store_sems = refs
     tokens = k_ref.shape[0]
     tiles = lane_tiles(width)
     half = tiles // 2
@@ -58,8 +58,18 @@
         for i, (array, ref) in enumerate(((keys, k_ref), (values, v_ref))):
             loads.append(pltpu.make_async_copy(array.at[:, at], ref.at[:, at], sems.at[c, i]))
             loads[-1].start()
+    mine = lax.axis_index(GROUP)
+    per = outs[0].shape[0]
+
+    def store(k, step):
+        return pltpu.make_async_copy(
+            held.at[pl.ds(k * per, per)], outs[step], store_sems.at[step]
+        )
+
     ones = jnp.ones((8, tokens), BF16)
-    held[tiles * HD :, :] = jnp.zeros((held.shape[0] - tiles * HD, LANE), F32)
+    groups = HD // 8
+    held[tiles * groups :] = jnp.zeros((held.shape[0] - tiles * groups, 8, LANE), F32)
+    sent = 0
     for j in range(tiles):
         if j in (0, half):
             for copy in loads[2 * (j // half) : 2 * (j // half) + 2]:
@@ -75,13 +85,16 @@
         for i in range(n // HD):
             packed = jnp.where(head == i, full[i * HD : (i + 1) * HD, :], packed)
         if n < LANE:
-            held[j * HD : (j + 1) * HD, :] = jnp.zeros((HD, LANE), F32)
-        held[j * HD : (j + 1) * HD, :n] = packed
-        held[tiles * HD + j : tiles * HD + j + 1, :n] = ksum[:1]
-    mine = lax.axis_index(GROUP)
-    for step, out in enumerate(outs):
-        rows = piece(target(mine, step, pieces), 8 * out.shape[0])
-        out[...] = held[rows, :].reshape(out.shape)
+            held[j * groups : (j + 1) * groups] = jnp.zeros((groups, 8, LANE), F32)
+        held[j * groups : (j + 1) * groups, :, :n] = packed.reshape(groups, 8, n)
+        held[tiles * groups + j // 8, j % 8 : j % 8 + 1, :n] = ksum[:1]
+        done = pieces if j == tiles - 1 else (j + 1) * groups // per
+        for k in range(sent, done):
+            for step in range(pieces):
+                pl.when(target(mine, step, pieces) == k)(store(k, step).start)
+        sent = done
+    for step in range(pieces):
+        store(0, step).wait()
 
 
 def halves(x):
@@ -369,12 +382,13 @@
         functools.partial(state_kernel, width, pieces),
         out_shape=[jax.ShapeDtypeStruct((per // 8, 8, LANE), F32)] * pieces,
         in_specs=[pl.BlockSpec(memory_space=pltpu.HBM)] * 2,
-        out_specs=whole(pieces),
+        out_specs=[pl.BlockSpec(memory_space=pl.ANY)] * pieces,
         scratch_shapes=[
             pltpu.VMEM((tokens, width), BF16),
             pltpu.VMEM((tokens, width), BF16),
-            pltpu.VMEM((pieces * per, LANE), F32),
+            pltpu.VMEM((pieces * per // 8, 8, LANE), F32),
             pltpu.SemaphoreType.DMA((2, 2)),
+            pltpu.SemaphoreType.DMA((pieces,)),
         ],
         compiler_params=pltpu.CompilerParams(vmem_limit_bytes=VMEM_MOST),
         cost_estimate=pl.CostEstimate(

time: 35.2 us -> 35.2 us (level)
  no operation moved by 1% of the time
where the time goes in v3:
time: 35.2 us; the launch traced here: 35 us
  starting transfers between devices  14.3 us (41%)
  Pallas kernels  8.96 us (25%)
  waiting for transfers between devices  8.13 us (23%)
  local copies, waits for them, and re-layouts  2.54 us (7%)
  between operations  0.82 us (2%)
    ppermute x6, starting transfers between devices, exchange(): lax.ppermute(value, GROUP, [(i, target(i, step, n)) for i in range(n)])  8.36 us
    pallas_call x2, Pallas kernels, convolve(): pl.pallas_call(kernel, out_shape=result, in_specs=whole(len(arrays)), out...  4.89 us
    ppermute x6, waiting for transfers between devices, exchange(): lax.ppermute(value, GROUP, [(i, target(i, step, n)) for i in range(n)])  4.26 us
    ppermute x2, waiting for transfers between devices, frame_prefix(): got = lax.ppermute(value, 'frame', pairs)  2.95 us
    ppermute x1, starting transfers between devices, across(): lax.ppermute(value, 'row_far', [(i, (i + step) % n) for i in range(n)])  2.59 us
    pallas_call x1, Pallas kernels, on_device(): pl.pallas_call(functools.partial(state_kernel, width, pieces), out_shape=...  2.51 us
    slice x1, local copies, waits for them, and re-layouts, halo_sends(): return (to_rows, sends(hidden[:, :, 0], hidden[:, :, cols - 1], 'col'))  2.41 us
    ppermute x2, starting transfers between devices, frame_prefix(): got = lax.ppermute(value, 'frame', pairs)  1.63 us
  transfers between devices with their start and end apart: 12, of which 7 were waited for; matrix products, arithmetic and copies ran while one was open for 7% of the time, Pallas kernels for 14%

profile of v3, /device:TPU:0, one launch (start us, length us, event | category | flops | bytes accessed | tf_op | source)
XLA Modules:
  0.0 35.0 jit_solution(377154132823879104)
XLA Ops:
  0.6 0.0 copy-start
  0.6 2.5 %local_state.1 = (f32[19,8,128]{2,1,0:T(8,128)}, f32[19,8,128]{2,1,0:T(8,128)}, f32[19,8,128]{2,1,0:T(8,128)}, f32[19,8,128]{2,1,0:T(8,128)}) custom-call(bf16[128,2240]{1,0:T(8,128)(2,1)} %bitcast.35, bf16[128,2240]{1,0:T(8,128)(2,1)} %bitcast.36), custom_call_target="tpu_custom_call" | custom-call | flops 18350080 | bytes 1720320 | tf_op jit(solution)/shard_map/local_state/pallas_call | solution.py:381
  3.2 3.0 %collective-permute-start = (f32[19,8,128]{2,1,0:T(8,128)}, f32[19,8,128]{2,1,0:T(8,128)S(1)}, u32[]{:S(2)}, u32[]{:S(2)}) collective-permute-start(f32[19,8,128]{2,1,0:T(8,128)} %get-tuple-element.22), channel_id=1, source_target_pairs={{0,1},{1,0},{2,3},{3,2},{4,5},{5,4},{6,7},{7,6},{8,9},{9,8},{10,11... | collective-permute-start | bytes 233480 | tf_op jit(solution)/shard_map/ppermute | solution.py:358
  6.2 1.6 %collective-permute-start.1 = (f32[19,8,128]{2,1,0:T(8,128)}, f32[19,8,128]{2,1,0:T(8,128)S(1)}, u32[]{:S(2)}, u32[]{:S(2)}) collective-permute-start(f32[19,8,128]{2,1,0:T(8,128)} %get-tuple-element.23), channel_id=1, source_target_pairs={{0,2},{1,3},{2,0},{3,1},{4,6},{5,7},{6,4},{7,5},{8,10},{9,11},{10,... | collective-permute-start | bytes 233480 | tf_op jit(solution)/shard_map/ppermute | solution.py:358
  7.8 0.0 collective-permute-start.2
  7.8 0.0 copy-start.4
  7.8 0.0 copy-start.1
  7.8 0.0 copy-start.3
  7.8 2.4 %fusion.3 = (bf16[2,8,1,5632]{3,2,1,0:T(2,128)(2,1)S(1)}, bf16[2,8,1,5632]{3,2,1,0:T(2,128)(2,1)S(1)}) fusion(bf16[2,8,8,5632]{3,2,1,0:T(8,128)(2,1)} %hidden.1), kind=kLoop, calls=%fused_computation.16 | loop fusion | bytes 720896 | tf_op jit(solution)/shard_map/slice | solution.py:290
  10.2 0.0 copy-done
  10.3 0.0 collective-permute-done
  10.3 1.1 %collective-permute-done.1 = f32[19,8,128]{2,1,0:T(8,128)S(1)} collective-permute-done((f32[19,8,128]{2,1,0:T(8,128)}, f32[19,8,128]{2,1,0:T(8,128)S(1)}, u32[]{:S(2)}, u32[]{:S(2)}) %collective-permute-start.1) | collective-permute-done | bytes 77856 | tf_op jit(solution)/shard_map/ppermute | solution.py:358
  11.5 1.8 %collective-permute-done.2 = f32[19,8,128]{2,1,0:T(8,128)S(1)} collective-permute-done((f32[19,8,128]{2,1,0:T(8,128)}, f32[19,8,128]{2,1,0:T(8,128)S(1)}, u32[]{:S(2)}, u32[]{:S(2)}) %collective-permute-start.2) | collective-permute-done | bytes 77856 | tf_op jit(solution)/shard_map/ppermute | solution.py:358
  13.3 0.0 copy-done.4
  13.3 0.6 %collective-permute-start.4 = (bf16[2,8,5632]{2,1,0:T(8,128)(2,1)S(1)}, bf16[2,8,5632]{2,1,0:T(8,128)(2,1)S(1)}, u32[]{:S(2)}, u32[]{:S(2)}) collective-permute-start(bf16[2,8,5632]{2,1,0:T(8,128)(2,1)S(1)} %fusion.2), channel_id=1, source_target_pairs={{0,1},{1,0},{2,3},{3,2},{4,5},{5,4},{6,7},{7,6},{8,9},{9,8},{10,11... | collective-permute-start | bytes 540680 | tf_op jit(solution)/shard_map/ppermute | solution.py:323
  13.9 2.6 %collective-permute-start.3 = (f32[19,8,128]{2,1,0:T(8,128)S(1)}, f32[19,8,128]{2,1,0:T(8,128)S(1)}, u32[]{:S(2)}, u32[]{:S(2)}) collective-permute-start(f32[19,8,128]{2,1,0:T(8,128)S(1)} %add_add_fusion), channel_id=1, source_target_pairs={{0,4},{4,0},{1,5},{5,1},{2,6},{6,2},{3,7},{7,3},{8,12},{12,8},{9,1... | collective-permute-start | bytes 233480 | tf_op jit(solution)/shard_map/ppermute | solution.py:351
  16.5 0.0 copy-done.1
  16.5 0.0 copy-done.3
  16.5 2.6 %conv_inner.1.inner = f32[2,8,8,5632]{3,2,1,0:T(8,128)S(1)} custom-call(bf16[2,8,8,5632]{3,2,1,0:T(8,128)(2,1)S(1)} %copy-done, f32[9,5632]{1,0:T(8,128)S(1)} %copy-done.1, f32[44,128]{1,0:T(8,128)S(1)} %bitcast.34), custom_call_target="tpu_custom_call" | custom-call | flops 14417920 | bytes 4325376 | tf_op jit(solution)/shard_map/conv_inner/pallas_call | solution.py:327
  19.1 0.9 %collective-permute-done.3 = f32[19,8,128]{2,1,0:T(8,128)S(1)} collective-permute-done((f32[19,8,128]{2,1,0:T(8,128)S(1)}, f32[19,8,128]{2,1,0:T(8,128)S(1)}, u32[]{:S(2)}, u32[]{:S(2)}) %collective-permute-start.3) | collective-permute-done | bytes 77856 | tf_op jit(solution)/shard_map/ppermute | solution.py:351
  20.0 0.0 collective-permute-done.4.col_e.col_o
  20.0 0.1 broadcast_select_fusion
  20.3 0.1 collective-permute-start.5
  20.4 0.5 %collective-permute-start.11 = (bf16[2,8,6400]{2,1,0:T(8,128)(2,1)S(1)}, bf16[2,8,6400]{2,1,0:T(8,128)(2,1)S(1)}, u32[]{:S(2)}, u32[]{:S(2)}) collective-permute-start(bf16[2,8,6400]{2,1,0:T(8,128)(2,1)S(1)} %pad_maximum_fusion.1), channel_id=1, source_target_pairs={{0,2},{2,0},{4,6},{6,4},{1,3},{3,1},{5,7},{7,5},{8,10},{10,8},{12,... | collective-permute-start | bytes 614408 | tf_op jit(solution)/shard_map/ppermute | solution.py:313
  20.9 0.7 %collective-permute-done.5 = f32[19,8,128]{2,1,0:T(8,128)S(1)} collective-permute-done((f32[19,8,128]{2,1,0:T(8,128)S(1)}, f32[19,8,128]{2,1,0:T(8,128)S(1)}, u32[]{:S(2)}, u32[]{:S(2)}) %collective-permute-start.5) | collective-permute-done | bytes 77856 | tf_op jit(solution)/shard_map/ppermute | solution.py:368
  21.6 1.6 %collective-permute-start.6 = (f32[19,8,128]{2,1,0:T(8,128)S(1)}, f32[19,8,128]{2,1,0:T(8,128)S(1)}, u32[]{:S(2)}, u32[]{:S(2)}) collective-permute-start(f32[19,8,128]{2,1,0:T(8,128)S(1)} %add.35), channel_id=1, source_target_pairs={{0,16},{8,24},{16,0},{24,8},{1,17},{9,25},{17,1},{25,9},{2,18},{10... | collective-permute-start | bytes 233480 | tf_op jit(solution)/shard_map/ppermute | solution.py:368
  23.2 0.7 %collective-permute-start.10 = (bf16[2,8,6400]{2,1,0:T(8,128)(2,1)S(1)}, bf16[2,8,6400]{2,1,0:T(8,128)(2,1)S(1)}, u32[]{:S(2)}, u32[]{:S(2)}) collective-permute-start(bf16[2,8,6400]{2,1,0:T(8,128)(2,1)S(1)} %pad_maximum_fusion), channel_id=1, source_target_pairs={{0,0},{2,4},{4,2},{6,6},{1,1},{3,5},{5,3},{7,7},{8,8},{10,12},{12,... | collective-permute-start | bytes 614408 | tf_op jit(solution)/shard_map/ppermute | solution.py:318
  23.9 2.2 %collective-permute-done.6 = f32[19,8,128]{2,1,0:T(8,128)S(1)} collective-permute-done((f32[19,8,128]{2,1,0:T(8,128)S(1)}, f32[19,8,128]{2,1,0:T(8,128)S(1)}, u32[]{:S(2)}, u32[]{:S(2)}) %collective-permute-start.6) | collective-permute-done | bytes 77856 | tf_op jit(solution)/shard_map/ppermute | solution.py:368
  26.1 0.0 copy-start.2
  26.1 2.4 %collective-permute-start.7 = (f32[19,8,128]{2,1,0:T(8,128)S(1)}, f32[19,8,128]{2,1,0:T(8,128)S(1)}, u32[]{:S(2)}, u32[]{:S(2)}) collective-permute-start(f32[19,8,128]{2,1,0:T(8,128)S(1)} %select_add_fusion.refs_3_), channel_id=1, source_target_pairs={{0,3},{1,2},{2,1},{3,0},{4,7},{5,6},{6,5},{7,4},{8,11},{9,10},{10,... | collective-permute-start | bytes 233480 | tf_op jit(solution)/shard_map/ppermute | solution.py:358
  28.5 0.6 %collective-permute-start.8 = (f32[19,8,128]{2,1,0:T(8,128)S(1)}, f32[19,8,128]{2,1,0:T(8,128)S(1)}, u32[]{:S(2)}, u32[]{:S(2)}) collective-permute-start(f32[19,8,128]{2,1,0:T(8,128)S(1)} %select_add_fusion.refs_3_), channel_id=1, source_target_pairs={{0,2},{1,3},{2,0},{3,1},{4,6},{5,7},{6,4},{7,5},{8,10},{9,11},{10,... | collective-permute-start | bytes 233480 | tf_op jit(solution)/shard_map/ppermute | solution.py:358
  29.1 0.8 %collective-permute-start.9 = (f32[19,8,128]{2,1,0:T(8,128)S(1)}, f32[19,8,128]{2,1,0:T(8,128)S(1)}, u32[]{:S(2)}, u32[]{:S(2)}) collective-permute-start(f32[19,8,128]{2,1,0:T(8,128)S(1)} %select_add_fusion.refs_3_), channel_id=1, source_target_pairs={{0,1},{1,0},{2,3},{3,2},{4,5},{5,4},{6,7},{7,6},{8,9},{9,8},{10,11... | collective-permute-start | bytes 233480 | tf_op jit(solution)/shard_map/ppermute | solution.py:358
  29.9 0.0 collective-permute-done.11.row_e
  29.9 0.0 collective-permute-done.10.row_o
  29.9 2.3 %conv_gate.1 = bf16[2,8,8,2816]{3,2,1,0:T(8,128)(2,1)} custom-call(f32[2,8,8,5632]{3,2,1,0:T(8,128)S(1)} %conv_inner.1.inner, bf16[2,8,6400]{2,1,0:T(8,128)(2,1)S(1)} %collective-permute-done.10.row_o, bf16[2,8,6400]{2,1,0:T(8,128)(2,1)S(1)} %collective-permute-done.11.row_e, bf16[2,8,5632]{2,1,0:T(8,128)(2,1)S(1)} %collective-permute-done.4.col_e.col_o, ...), custom_call_target="tpu_custom_call" | custom-call | flops 7208960 | bytes 2162688 | tf_op jit(solution)/shard_map/conv_gate/pallas_call | solution.py:327
  32.1 0.0 collective-permute-done.7.refs_0_
  32.2 0.7 %collective-permute-done.8.refs_1_ = f32[19,8,128]{2,1,0:T(8,128)S(1)} collective-permute-done((f32[19,8,128]{2,1,0:T(8,128)S(1)}, f32[19,8,128]{2,1,0:T(8,128)S(1)}, u32[]{:S(2)}, u32[]{:S(2)}) %collective-permute-start.8) | collective-permute-done | bytes 77856 | tf_op jit(solution)/shard_map/ppermute | solution.py:358
  32.9 0.6 %collective-permute-done.9.refs_2_ = f32[19,8,128]{2,1,0:T(8,128)S(1)} collective-permute-done((f32[19,8,128]{2,1,0:T(8,128)S(1)}, f32[19,8,128]{2,1,0:T(8,128)S(1)}, u32[]{:S(2)}, u32[]{:S(2)}) %collective-permute-start.9) | collective-permute-done | bytes 77856 | tf_op jit(solution)/shard_map/ppermute | solution.py:358
  33.5 0.0 copy-done.2
  33.5 1.6 %attend.1 = bf16[128,2240]{1,0:T(8,128)(2,1)} custom-call(bf16[128,2240]{1,0:T(8,128)(2,1)S(1)} %bitcast.33, f32[19,8,128]{2,1,0:T(8,128)S(1)} %collective-permute-done.7.refs_0_, f32[19,8,128]{2,1,0:T(8,128)S(1)} %collective-permute-done.8.refs_1_, f32[19,8,128]{2,1,0:T(8,128)S(1)} %collective-permute-done.9.refs_2_, f32[19,8,128]{2,1,0:T(8,128)S(1)} %select_add_fusion.refs_3_), custom_call_target="tpu_custom_call" | custom-call | flops 73400320 | bytes 1720320 | tf_op jit(solution)/shard_map/attend/pallas_call | solution.py:420
  (13 shorter events, 0.3 us)
Async XLA Ops:
  0.6 9.6 %copy-start = (bf16[2,8,8,5632]{3,2,1,0:T(8,128)(2,1)S(1)}, bf16[2,8,8,5632]{3,2,1,0:T(8,128)(2,1)}, u32[]{:S(2)}) copy-start(bf16[2,8,8,5632]{3,2,1,0:T(8,128)(2,1)} %hidden.1) | copy-start | bytes 4325380
  3.2 7.2 %collective-permute-start = (f32[19,8,128]{2,1,0:T(8,128)}, f32[19,8,128]{2,1,0:T(8,128)S(1)}, u32[]{:S(2)}, u32[]{:S(2)}) collective-permute-start(f32[19,8,128]{2,1,0:T(8,128)} %get-tuple-element.22), channel_id=1, source_target_pairs={{0,1},{1,0},{2,3},{3,2},{4,5},{5,4},{6,7},{7,6},{8,9},{9,8},{10,11... | collective-permute-start | bytes 233480 | tf_op jit(solution)/shard_map/ppermute | solution.py:358
  6.2 5.3 %collective-permute-start.1 = (f32[19,8,128]{2,1,0:T(8,128)}, f32[19,8,128]{2,1,0:T(8,128)S(1)}, u32[]{:S(2)}, u32[]{:S(2)}) collective-permute-start(f32[19,8,128]{2,1,0:T(8,128)} %get-tuple-element.23), channel_id=1, source_target_pairs={{0,2},{1,3},{2,0},{3,1},{4,6},{5,7},{6,4},{7,5},{8,10},{9,11},{10,... | collective-permute-start | bytes 233480 | tf_op jit(solution)/shard_map/ppermute | solution.py:358
  7.8 5.5 %collective-permute-start.2 = (f32[19,8,128]{2,1,0:T(8,128)}, f32[19,8,128]{2,1,0:T(8,128)S(1)}, u32[]{:S(2)}, u32[]{:S(2)}) collective-permute-start(f32[19,8,128]{2,1,0:T(8,128)} %get-tuple-element.24), channel_id=1, source_target_pairs={{0,3},{1,2},{2,1},{3,0},{4,7},{5,6},{6,5},{7,4},{8,11},{9,10},{10,... | collective-permute-start | bytes 233480 | tf_op jit(solution)/shard_map/ppermute | solution.py:358
  7.8 5.5 %copy-start.4 = (f32[19,8,128]{2,1,0:T(8,128)S(1)}, f32[19,8,128]{2,1,0:T(8,128)}, u32[]{:S(2)}) copy-start(f32[19,8,128]{2,1,0:T(8,128)} %get-tuple-element.21) | copy-start | bytes 233476
  7.8 8.7 %copy-start.1 = (f32[9,5632]{1,0:T(8,128)S(1)}, f32[9,5632]{1,0:T(8,128)}, u32[]{:S(2)}) copy-start(f32[9,5632]{1,0:T(8,128)} %weight.3) | copy-start | bytes 608260
  7.8 8.7 %copy-start.3 = (f32[5632]{0:T(1024)S(1)}, f32[5632]{0:T(1024)}, u32[]{:S(2)}) copy-start(f32[5632]{0:T(1024)} %param.11) | copy-start | bytes 67588
  13.3 6.7 %collective-permute-start.4 = (bf16[2,8,5632]{2,1,0:T(8,128)(2,1)S(1)}, bf16[2,8,5632]{2,1,0:T(8,128)(2,1)S(1)}, u32[]{:S(2)}, u32[]{:S(2)}) collective-permute-start(bf16[2,8,5632]{2,1,0:T(8,128)(2,1)S(1)} %fusion.2), channel_id=1, source_target_pairs={{0,1},{1,0},{2,3},{3,2},{4,5},{5,4},{6,7},{7,6},{8,9},{9,8},{10,11... | collective-permute-start | bytes 540680 | tf_op jit(solution)/shard_map/ppermute | solution.py:323
  13.9 6.1 %collective-permute-start.3 = (f32[19,8,128]{2,1,0:T(8,128)S(1)}, f32[19,8,128]{2,1,0:T(8,128)S(1)}, u32[]{:S(2)}, u32[]{:S(2)}) collective-permute-start(f32[19,8,128]{2,1,0:T(8,128)S(1)} %add_add_fusion), channel_id=1, source_target_pairs={{0,4},{4,0},{1,5},{5,1},{2,6},{6,2},{3,7},{7,3},{8,12},{12,8},{9,1... | collective-permute-start | bytes 233480 | tf_op jit(solution)/shard_map/ppermute | solution.py:351
  20.3 1.3 %collective-permute-start.5 = (f32[19,8,128]{2,1,0:T(8,128)S(1)}, f32[19,8,128]{2,1,0:T(8,128)S(1)}, u32[]{:S(2)}, u32[]{:S(2)}) collective-permute-start(f32[19,8,128]{2,1,0:T(8,128)S(1)} %add.33), channel_id=1, source_target_pairs={{0,8},{8,0},{16,24},{24,16},{1,9},{9,1},{17,25},{25,17},{2,10},{10... | collective-permute-start | bytes 233480 | tf_op jit(solution)/shard_map/ppermute | solution.py:368
  20.4 9.5 %collective-permute-start.11 = (bf16[2,8,6400]{2,1,0:T(8,128)(2,1)S(1)}, bf16[2,8,6400]{2,1,0:T(8,128)(2,1)S(1)}, u32[]{:S(2)}, u32[]{:S(2)}) collective-permute-start(bf16[2,8,6400]{2,1,0:T(8,128)(2,1)S(1)} %pad_maximum_fusion.1), channel_id=1, source_target_pairs={{0,2},{2,0},{4,6},{6,4},{1,3},{3,1},{5,7},{7,5},{8,10},{10,8},{12,... | collective-permute-start | bytes 614408 | tf_op jit(solution)/shard_map/ppermute | solution.py:313
  21.6 4.5 %collective-permute-start.6 = (f32[19,8,128]{2,1,0:T(8,128)S(1)}, f32[19,8,128]{2,1,0:T(8,128)S(1)}, u32[]{:S(2)}, u32[]{:S(2)}) collective-permute-start(f32[19,8,128]{2,1,0:T(8,128)S(1)} %add.35), channel_id=1, source_target_pairs={{0,16},{8,24},{16,0},{24,8},{1,17},{9,25},{17,1},{25,9},{2,18},{10... | collective-permute-start | bytes 233480 | tf_op jit(solution)/shard_map/ppermute | solution.py:368
  23.2 6.7 %collective-permute-start.10 = (bf16[2,8,6400]{2,1,0:T(8,128)(2,1)S(1)}, bf16[2,8,6400]{2,1,0:T(8,128)(2,1)S(1)}, u32[]{:S(2)}, u32[]{:S(2)}) collective-permute-start(bf16[2,8,6400]{2,1,0:T(8,128)(2,1)S(1)} %pad_maximum_fusion), channel_id=1, source_target_pairs={{0,0},{2,4},{4,2},{6,6},{1,1},{3,5},{5,3},{7,7},{8,8},{10,12},{12,... | collective-permute-start | bytes 614408 | tf_op jit(solution)/shard_map/ppermute | solution.py:318
  26.1 7.4 %copy-start.2 = (bf16[2,8,8,2240]{3,2,1,0:T(8,128)(2,1)S(1)}, bf16[2,8,8,2240]{3,2,1,0:T(8,128)(2,1)}, u32[]{:S(2)}) copy-start(bf16[2,8,8,2240]{3,2,1,0:T(8,128)(2,1)} %param.6) | copy-start | bytes 1720324
  26.1 6.0 %collective-permute-start.7 = (f32[19,8,128]{2,1,0:T(8,128)S(1)}, f32[19,8,128]{2,1,0:T(8,128)S(1)}, u32[]{:S(2)}, u32[]{:S(2)}) collective-permute-start(f32[19,8,128]{2,1,0:T(8,128)S(1)} %select_add_fusion.refs_3_), channel_id=1, source_target_pairs={{0,3},{1,2},{2,1},{3,0},{4,7},{5,6},{6,5},{7,4},{8,11},{9,10},{10,... | collective-permute-start | bytes 233480 | tf_op jit(solution)/shard_map/ppermute | solution.py:358
  28.5 4.4 %collective-permute-start.8 = (f32[19,8,128]{2,1,0:T(8,128)S(1)}, f32[19,8,128]{2,1,0:T(8,128)S(1)}, u32[]{:S(2)}, u32[]{:S(2)}) collective-permute-start(f32[19,8,128]{2,1,0:T(8,128)S(1)} %select_add_fusion.refs_3_), channel_id=1, source_target_pairs={{0,2},{1,3},{2,0},{3,1},{4,6},{5,7},{6,4},{7,5},{8,10},{9,11},{10,... | collective-permute-start | bytes 233480 | tf_op jit(solution)/shard_map/ppermute | solution.py:358
  29.1 4.4 %collective-permute-start.9 = (f32[19,8,128]{2,1,0:T(8,128)S(1)}, f32[19,8,128]{2,1,0:T(8,128)S(1)}, u32[]{:S(2)}, u32[]{:S(2)}) collective-permute-start(f32[19,8,128]{2,1,0:T(8,128)S(1)} %select_add_fusion.refs_3_), channel_id=1, source_target_pairs={{0,1},{1,0},{2,3},{3,2},{4,5},{5,4},{6,7},{7,6},{8,9},{9,8},{10,11... | collective-permute-start | bytes 233480 | tf_op jit(solution)/shard_map/ppermute | solution.py:358

commit v4 on v2

--- a/solution.py
+++ b/solution.py
@@ -383,7 +383,7 @@
         name="local_state",
     )(keys.reshape(tokens, width), values.reshape(tokens, width))
 
-    near = sum((exchange(local[step], step) for step in range(1, pieces)), local[0])
+    near = sum((exchange(local[step], step) for step in range(pieces - 1, 0, -1)), local[0])
     near, (to_rows, to_cols), bias = lax.optimization_barrier(
         (near, halo_sends(hidden), conv_bias)
     )

time: 35.2 us -> 34.8 us (0.989)
  waiting for transfers between devices: 8.11 us -> 5.54 us
  starting transfers between devices: 14.3 us -> 16.5 us
    ppermute x1, starting transfers between devices: 0.48 us -> 1.65 us  [swap_even_rows(): return lax.ppermute(to_even, ROW, swaps(lax.axis_size(ROW))[0])]
    ppermute x6, waiting for transfers between devices: 4.25 us -> 3.18 us  [exchange(): lax.ppermute(value, GROUP, [(i, target(i, step, n)) for i in range(n)])]
    ppermute x1, waiting for transfers between devices: 0.91 us -> 0.08 us  [across(): lax.ppermute(value, 'row_far', [(i, (i + step) % n) for i in range(n)])]
    ppermute x6, starting transfers between devices: 8.36 us -> 9.06 us  [exchange(): lax.ppermute(value, GROUP, [(i, target(i, step, n)) for i in range(n)])]
    ppermute x2, waiting for transfers between devices: 2.94 us -> 2.28 us  [frame_prefix(): got = lax.ppermute(value, 'frame', pairs)]
  transfers between devices with their start and end apart: 12 -> 12, of which waited for: 7 -> 5; matrix products, arithmetic and copies ran while one was open for 7% -> 7% of each run, Pallas kernels for 14% -> 14%
where the time goes in v4:
time: 34.8 us; the launch traced here: 34.7 us
  starting transfers between devices  16.5 us (47%)
  Pallas kernels  9.01 us (26%)
  waiting for transfers between devices  5.54 us (16%)
  local copies, waits for them, and re-layouts  2.54 us (7%)
  between operations  0.83 us (2%)
    ppermute x6, starting transfers between devices, exchange(): lax.ppermute(value, GROUP, [(i, target(i, step, n)) for i in range(n)])  9.06 us
    pallas_call x2, Pallas kernels, convolve(): pl.pallas_call(kernel, out_shape=result, in_specs=whole(len(arrays)), out...  4.89 us
    ppermute x6, waiting for transfers between devices, exchange(): lax.ppermute(value, GROUP, [(i, target(i, step, n)) for i in range(n)])  3.18 us
    ppermute x1, starting transfers between devices, across(): lax.ppermute(value, 'row_far', [(i, (i + step) % n) for i in range(n)])  2.59 us
    pallas_call x1, Pallas kernels, on_device(): pl.pallas_call(functools.partial(state_kernel, width, pieces), out_shape=...  2.56 us
    slice x1, local copies, waits for them, and re-layouts, halo_sends(): return (to_rows, sends(hidden[:, :, 0], hidden[:, :, cols - 1], 'col'))  2.41 us
    ppermute x2, waiting for transfers between devices, frame_prefix(): got = lax.ppermute(value, 'frame', pairs)  2.28 us
    ppermute x1, starting transfers between devices, swap_even_rows(): return lax.ppermute(to_even, ROW, swaps(lax.axis_size(ROW))[0])  1.65 us
  transfers between devices with their start and end apart: 12, of which 5 were waited for; matrix products, arithmetic and copies ran while one was open for 7% of the time, Pallas kernels for 14%

profile of v4, /device:TPU:0, one launch (start us, length us, event | category | flops | bytes accessed | tf_op | source)
XLA Modules:
  0.0 34.7 jit_solution(13612586454471845833)
XLA Ops:
  0.6 0.0 copy-start
  0.6 2.6 %local_state.1 = (f32[19,8,128]{2,1,0:T(8,128)}, f32[19,8,128]{2,1,0:T(8,128)}, f32[19,8,128]{2,1,0:T(8,128)}, f32[19,8,128]{2,1,0:T(8,128)}) custom-call(bf16[128,2240]{1,0:T(8,128)(2,1)} %bitcast.35, bf16[128,2240]{1,0:T(8,128)(2,1)} %bitcast.36), custom_call_target="tpu_custom_call" | custom-call | flops 18350080 | bytes 1720320 | tf_op jit(solution)/shard_map/local_state/pallas_call | solution.py:368
  3.2 4.0 %collective-permute-start = (f32[19,8,128]{2,1,0:T(8,128)}, f32[19,8,128]{2,1,0:T(8,128)S(1)}, u32[]{:S(2)}, u32[]{:S(2)}) collective-permute-start(f32[19,8,128]{2,1,0:T(8,128)} %get-tuple-element.22), channel_id=1, source_target_pairs={{0,3},{1,2},{2,1},{3,0},{4,7},{5,6},{6,5},{7,4},{8,11},{9,10},{10,... | collective-permute-start | bytes 233480 | tf_op jit(solution)/shard_map/ppermute | solution.py:345
  7.3 0.4 %collective-permute-start.1 = (f32[19,8,128]{2,1,0:T(8,128)}, f32[19,8,128]{2,1,0:T(8,128)S(1)}, u32[]{:S(2)}, u32[]{:S(2)}) collective-permute-start(f32[19,8,128]{2,1,0:T(8,128)} %get-tuple-element.23), channel_id=1, source_target_pairs={{0,2},{1,3},{2,0},{3,1},{4,6},{5,7},{6,4},{7,5},{8,10},{9,11},{10,... | collective-permute-start | bytes 233480 | tf_op jit(solution)/shard_map/ppermute | solution.py:345
  7.7 0.2 collective-permute-start.2
  7.9 0.0 copy-start.4
  7.9 0.0 copy-start.1
  7.9 0.0 copy-start.3
  7.9 2.4 %fusion.3 = (bf16[2,8,1,5632]{3,2,1,0:T(2,128)(2,1)S(1)}, bf16[2,8,1,5632]{3,2,1,0:T(2,128)(2,1)S(1)}) fusion(bf16[2,8,8,5632]{3,2,1,0:T(8,128)(2,1)} %hidden.1), kind=kLoop, calls=%fused_computation.16 | loop fusion | bytes 720896 | tf_op jit(solution)/shard_map/slice | solution.py:277
  10.3 0.0 copy-done
  10.4 0.0 collective-permute-done
  10.4 1.5 %collective-permute-done.1 = f32[19,8,128]{2,1,0:T(8,128)S(1)} collective-permute-done((f32[19,8,128]{2,1,0:T(8,128)}, f32[19,8,128]{2,1,0:T(8,128)S(1)}, u32[]{:S(2)}, u32[]{:S(2)}) %collective-permute-start.1) | collective-permute-done | bytes 77856 | tf_op jit(solution)/shard_map/ppermute | solution.py:345
  12.0 0.4 %collective-permute-done.2 = f32[19,8,128]{2,1,0:T(8,128)S(1)} collective-permute-done((f32[19,8,128]{2,1,0:T(8,128)}, f32[19,8,128]{2,1,0:T(8,128)S(1)}, u32[]{:S(2)}, u32[]{:S(2)}) %collective-permute-start.2) | collective-permute-done | bytes 77856 | tf_op jit(solution)/shard_map/ppermute | solution.py:345
  12.3 0.0 copy-done.4
  12.3 0.9 %collective-permute-start.4 = (bf16[2,8,5632]{2,1,0:T(8,128)(2,1)S(1)}, bf16[2,8,5632]{2,1,0:T(8,128)(2,1)S(1)}, u32[]{:S(2)}, u32[]{:S(2)}) collective-permute-start(bf16[2,8,5632]{2,1,0:T(8,128)(2,1)S(1)} %fusion.2), channel_id=1, source_target_pairs={{0,1},{1,0},{2,3},{3,2},{4,5},{5,4},{6,7},{7,6},{8,9},{9,8},{10,11... | collective-permute-start | bytes 540680 | tf_op jit(solution)/shard_map/ppermute | solution.py:310
  13.2 2.6 %collective-permute-start.3 = (f32[19,8,128]{2,1,0:T(8,128)S(1)}, f32[19,8,128]{2,1,0:T(8,128)S(1)}, u32[]{:S(2)}, u32[]{:S(2)}) collective-permute-start(f32[19,8,128]{2,1,0:T(8,128)S(1)} %add_add_fusion), channel_id=1, source_target_pairs={{0,4},{4,0},{1,5},{5,1},{2,6},{6,2},{3,7},{7,3},{8,12},{12,8},{9,1... | collective-permute-start | bytes 233480 | tf_op jit(solution)/shard_map/ppermute | solution.py:338
  15.8 0.0 copy-done.1
  15.8 0.0 copy-done.3
  15.8 2.6 %conv_inner.1.inner = f32[2,8,8,5632]{3,2,1,0:T(8,128)S(1)} custom-call(bf16[2,8,8,5632]{3,2,1,0:T(8,128)(2,1)S(1)} %copy-done, f32[9,5632]{1,0:T(8,128)S(1)} %copy-done.1, f32[44,128]{1,0:T(8,128)S(1)} %bitcast.34), custom_call_target="tpu_custom_call" | custom-call | flops 14417920 | bytes 4325376 | tf_op jit(solution)/shard_map/conv_inner/pallas_call | solution.py:314
  18.4 0.1 collective-permute-done.3
  18.5 0.0 collective-permute-done.4.col_e.col_o
  18.5 0.1 broadcast_select_fusion
  18.7 0.1 collective-permute-start.5
  18.8 1.6 %collective-permute-start.11 = (bf16[2,8,6400]{2,1,0:T(8,128)(2,1)S(1)}, bf16[2,8,6400]{2,1,0:T(8,128)(2,1)S(1)}, u32[]{:S(2)}, u32[]{:S(2)}) collective-permute-start(bf16[2,8,6400]{2,1,0:T(8,128)(2,1)S(1)} %pad_maximum_fusion.1), channel_id=1, source_target_pairs={{0,2},{2,0},{4,6},{6,4},{1,3},{3,1},{5,7},{7,5},{8,10},{10,8},{12,... | collective-permute-start | bytes 614408 | tf_op jit(solution)/shard_map/ppermute | solution.py:300
  20.5 0.0 collective-permute-done.5
  20.6 1.6 %collective-permute-start.6 = (f32[19,8,128]{2,1,0:T(8,128)S(1)}, f32[19,8,128]{2,1,0:T(8,128)S(1)}, u32[]{:S(2)}, u32[]{:S(2)}) collective-permute-start(f32[19,8,128]{2,1,0:T(8,128)S(1)} %add.35), channel_id=1, source_target_pairs={{0,16},{8,24},{16,0},{24,8},{1,17},{9,25},{17,1},{25,9},{2,18},{10... | collective-permute-start | bytes 233480 | tf_op jit(solution)/shard_map/ppermute | solution.py:355
  22.1 0.7 %collective-permute-start.10 = (bf16[2,8,6400]{2,1,0:T(8,128)(2,1)S(1)}, bf16[2,8,6400]{2,1,0:T(8,128)(2,1)S(1)}, u32[]{:S(2)}, u32[]{:S(2)}) collective-permute-start(bf16[2,8,6400]{2,1,0:T(8,128)(2,1)S(1)} %pad_maximum_fusion), channel_id=1, source_target_pairs={{0,0},{2,4},{4,2},{6,6},{1,1},{3,5},{5,3},{7,7},{8,8},{10,12},{12,... | collective-permute-start | bytes 614408 | tf_op jit(solution)/shard_map/ppermute | solution.py:305
  22.8 2.3 %collective-permute-done.6 = f32[19,8,128]{2,1,0:T(8,128)S(1)} collective-permute-done((f32[19,8,128]{2,1,0:T(8,128)S(1)}, f32[19,8,128]{2,1,0:T(8,128)S(1)}, u32[]{:S(2)}, u32[]{:S(2)}) %collective-permute-start.6) | collective-permute-done | bytes 77856 | tf_op jit(solution)/shard_map/ppermute | solution.py:355
  25.1 0.0 copy-start.2
  25.1 3.6 %collective-permute-start.7 = (f32[19,8,128]{2,1,0:T(8,128)S(1)}, f32[19,8,128]{2,1,0:T(8,128)S(1)}, u32[]{:S(2)}, u32[]{:S(2)}) collective-permute-start(f32[19,8,128]{2,1,0:T(8,128)S(1)} %select_add_fusion.refs_3_), channel_id=1, source_target_pairs={{0,3},{1,2},{2,1},{3,0},{4,7},{5,6},{6,5},{7,4},{8,11},{9,10},{10,... | collective-permute-start | bytes 233480 | tf_op jit(solution)/shard_map/ppermute | solution.py:345
  28.7 0.0 collective-permute-start.8
  28.7 0.8 %collective-permute-start.9 = (f32[19,8,128]{2,1,0:T(8,128)S(1)}, f32[19,8,128]{2,1,0:T(8,128)S(1)}, u32[]{:S(2)}, u32[]{:S(2)}) collective-permute-start(f32[19,8,128]{2,1,0:T(8,128)S(1)} %select_add_fusion.refs_3_), channel_id=1, source_target_pairs={{0,1},{1,0},{2,3},{3,2},{4,5},{5,4},{6,7},{7,6},{8,9},{9,8},{10,11... | collective-permute-start | bytes 233480 | tf_op jit(solution)/shard_map/ppermute | solution.py:345
  29.5 0.0 collective-permute-done.11.row_e
  29.5 0.0 collective-permute-done.10.row_o
  29.5 2.3 %conv_gate.1 = bf16[2,8,8,2816]{3,2,1,0:T(8,128)(2,1)} custom-call(f32[2,8,8,5632]{3,2,1,0:T(8,128)S(1)} %conv_inner.1.inner, bf16[2,8,6400]{2,1,0:T(8,128)(2,1)S(1)} %collective-permute-done.10.row_o, bf16[2,8,6400]{2,1,0:T(8,128)(2,1)S(1)} %collective-permute-done.11.row_e, bf16[2,8,5632]{2,1,0:T(8,128)(2,1)S(1)} %collective-permute-done.4.col_e.col_o, ...), custom_call_target="tpu_custom_call" | custom-call | flops 7208960 | bytes 2162688 | tf_op jit(solution)/shard_map/conv_gate/pallas_call | solution.py:314
  31.8 0.0 collective-permute-done.7.refs_0_
  31.8 1.3 %collective-permute-done.8.refs_1_ = f32[19,8,128]{2,1,0:T(8,128)S(1)} collective-permute-done((f32[19,8,128]{2,1,0:T(8,128)S(1)}, f32[19,8,128]{2,1,0:T(8,128)S(1)}, u32[]{:S(2)}, u32[]{:S(2)}) %collective-permute-start.8) | collective-permute-done | bytes 77856 | tf_op jit(solution)/shard_map/ppermute | solution.py:345
  33.1 0.0 collective-permute-done.9.refs_2_
  33.1 0.0 copy-done.2
  33.1 1.6 %attend.1 = bf16[128,2240]{1,0:T(8,128)(2,1)} custom-call(bf16[128,2240]{1,0:T(8,128)(2,1)S(1)} %bitcast.33, f32[19,8,128]{2,1,0:T(8,128)S(1)} %collective-permute-done.7.refs_0_, f32[19,8,128]{2,1,0:T(8,128)S(1)} %collective-permute-done.8.refs_1_, f32[19,8,128]{2,1,0:T(8,128)S(1)} %collective-permute-done.9.refs_2_, f32[19,8,128]{2,1,0:T(8,128)S(1)} %select_add_fusion.refs_3_), custom_call_target="tpu_custom_call" | custom-call | flops 73400320 | bytes 1720320 | tf_op jit(solution)/shard_map/attend/pallas_call | solution.py:406
  (13 shorter events, 0.3 us)
Async XLA Ops:
  0.6 9.7 %copy-start = (bf16[2,8,8,5632]{3,2,1,0:T(8,128)(2,1)S(1)}, bf16[2,8,8,5632]{3,2,1,0:T(8,128)(2,1)}, u32[]{:S(2)}) copy-start(bf16[2,8,8,5632]{3,2,1,0:T(8,128)(2,1)} %hidden.1) | copy-start | bytes 4325380
  3.2 7.2 %collective-permute-start = (f32[19,8,128]{2,1,0:T(8,128)}, f32[19,8,128]{2,1,0:T(8,128)S(1)}, u32[]{:S(2)}, u32[]{:S(2)}) collective-permute-start(f32[19,8,128]{2,1,0:T(8,128)} %get-tuple-element.22), channel_id=1, source_target_pairs={{0,3},{1,2},{2,1},{3,0},{4,7},{5,6},{6,5},{7,4},{8,11},{9,10},{10,... | collective-permute-start | bytes 233480 | tf_op jit(solution)/shard_map/ppermute | solution.py:345
  7.3 4.7 %collective-permute-start.1 = (f32[19,8,128]{2,1,0:T(8,128)}, f32[19,8,128]{2,1,0:T(8,128)S(1)}, u32[]{:S(2)}, u32[]{:S(2)}) collective-permute-start(f32[19,8,128]{2,1,0:T(8,128)} %get-tuple-element.23), channel_id=1, source_target_pairs={{0,2},{1,3},{2,0},{3,1},{4,6},{5,7},{6,4},{7,5},{8,10},{9,11},{10,... | collective-permute-start | bytes 233480 | tf_op jit(solution)/shard_map/ppermute | solution.py:345
  7.7 4.6 %collective-permute-start.2 = (f32[19,8,128]{2,1,0:T(8,128)}, f32[19,8,128]{2,1,0:T(8,128)S(1)}, u32[]{:S(2)}, u32[]{:S(2)}) collective-permute-start(f32[19,8,128]{2,1,0:T(8,128)} %get-tuple-element.24), channel_id=1, source_target_pairs={{0,1},{1,0},{2,3},{3,2},{4,5},{5,4},{6,7},{7,6},{8,9},{9,8},{10,11... | collective-permute-start | bytes 233480 | tf_op jit(solution)/shard_map/ppermute | solution.py:345
  7.9 4.4 %copy-start.4 = (f32[19,8,128]{2,1,0:T(8,128)S(1)}, f32[19,8,128]{2,1,0:T(8,128)}, u32[]{:S(2)}) copy-start(f32[19,8,128]{2,1,0:T(8,128)} %get-tuple-element.21) | copy-start | bytes 233476
  7.9 7.9 %copy-start.1 = (f32[9,5632]{1,0:T(8,128)S(1)}, f32[9,5632]{1,0:T(8,128)}, u32[]{:S(2)}) copy-start(f32[9,5632]{1,0:T(8,128)} %weight.3) | copy-start | bytes 608260
  7.9 7.9 %copy-start.3 = (f32[5632]{0:T(1024)S(1)}, f32[5632]{0:T(1024)}, u32[]{:S(2)}) copy-start(f32[5632]{0:T(1024)} %param.11) | copy-start | bytes 67588
  12.3 6.2 %collective-permute-start.4 = (bf16[2,8,5632]{2,1,0:T(8,128)(2,1)S(1)}, bf16[2,8,5632]{2,1,0:T(8,128)(2,1)S(1)}, u32[]{:S(2)}, u32[]{:S(2)}) collective-permute-start(bf16[2,8,5632]{2,1,0:T(8,128)(2,1)S(1)} %fusion.2), channel_id=1, source_target_pairs={{0,1},{1,0},{2,3},{3,2},{4,5},{5,4},{6,7},{7,6},{8,9},{9,8},{10,11... | collective-permute-start | bytes 540680 | tf_op jit(solution)/shard_map/ppermute | solution.py:310
  13.2 5.3 %collective-permute-start.3 = (f32[19,8,128]{2,1,0:T(8,128)S(1)}, f32[19,8,128]{2,1,0:T(8,128)S(1)}, u32[]{:S(2)}, u32[]{:S(2)}) collective-permute-start(f32[19,8,128]{2,1,0:T(8,128)S(1)} %add_add_fusion), channel_id=1, source_target_pairs={{0,4},{4,0},{1,5},{5,1},{2,6},{6,2},{3,7},{7,3},{8,12},{12,8},{9,1... | collective-permute-start | bytes 233480 | tf_op jit(solution)/shard_map/ppermute | solution.py:338
  18.7 1.8 %collective-permute-start.5 = (f32[19,8,128]{2,1,0:T(8,128)S(1)}, f32[19,8,128]{2,1,0:T(8,128)S(1)}, u32[]{:S(2)}, u32[]{:S(2)}) collective-permute-start(f32[19,8,128]{2,1,0:T(8,128)S(1)} %add.33), channel_id=1, source_target_pairs={{0,8},{8,0},{16,24},{24,16},{1,9},{9,1},{17,25},{25,17},{2,10},{10... | collective-permute-start | bytes 233480 | tf_op jit(solution)/shard_map/ppermute | solution.py:355
  18.8 10.7 %collective-permute-start.11 = (bf16[2,8,6400]{2,1,0:T(8,128)(2,1)S(1)}, bf16[2,8,6400]{2,1,0:T(8,128)(2,1)S(1)}, u32[]{:S(2)}, u32[]{:S(2)}) collective-permute-start(bf16[2,8,6400]{2,1,0:T(8,128)(2,1)S(1)} %pad_maximum_fusion.1), channel_id=1, source_target_pairs={{0,2},{2,0},{4,6},{6,4},{1,3},{3,1},{5,7},{7,5},{8,10},{10,8},{12,... | collective-permute-start | bytes 614408 | tf_op jit(solution)/shard_map/ppermute | solution.py:300
  20.6 4.5 %collective-permute-start.6 = (f32[19,8,128]{2,1,0:T(8,128)S(1)}, f32[19,8,128]{2,1,0:T(8,128)S(1)}, u32[]{:S(2)}, u32[]{:S(2)}) collective-permute-start(f32[19,8,128]{2,1,0:T(8,128)S(1)} %add.35), channel_id=1, source_target_pairs={{0,16},{8,24},{16,0},{24,8},{1,17},{9,25},{17,1},{25,9},{2,18},{10... | collective-permute-start | bytes 233480 | tf_op jit(solution)/shard_map/ppermute | solution.py:355
  22.1 7.4 %collective-permute-start.10 = (bf16[2,8,6400]{2,1,0:T(8,128)(2,1)S(1)}, bf16[2,8,6400]{2,1,0:T(8,128)(2,1)S(1)}, u32[]{:S(2)}, u32[]{:S(2)}) collective-permute-start(bf16[2,8,6400]{2,1,0:T(8,128)(2,1)S(1)} %pad_maximum_fusion), channel_id=1, source_target_pairs={{0,0},{2,4},{4,2},{6,6},{1,1},{3,5},{5,3},{7,7},{8,8},{10,12},{12,... | collective-permute-start | bytes 614408 | tf_op jit(solution)/shard_map/ppermute | solution.py:305
  25.1 8.0 %copy-start.2 = (bf16[2,8,8,2240]{3,2,1,0:T(8,128)(2,1)S(1)}, bf16[2,8,8,2240]{3,2,1,0:T(8,128)(2,1)}, u32[]{:S(2)}) copy-start(bf16[2,8,8,2240]{3,2,1,0:T(8,128)(2,1)} %param.6) | copy-start | bytes 1720324
  25.1 6.7 %collective-permute-start.7 = (f32[19,8,128]{2,1,0:T(8,128)S(1)}, f32[19,8,128]{2,1,0:T(8,128)S(1)}, u32[]{:S(2)}, u32[]{:S(2)}) collective-permute-start(f32[19,8,128]{2,1,0:T(8,128)S(1)} %select_add_fusion.refs_3_), channel_id=1, source_target_pairs={{0,3},{1,2},{2,1},{3,0},{4,7},{5,6},{6,5},{7,4},{8,11},{9,10},{10,... | collective-permute-start | bytes 233480 | tf_op jit(solution)/shard_map/ppermute | solution.py:345
  28.7 4.4 %collective-permute-start.8 = (f32[19,8,128]{2,1,0:T(8,128)S(1)}, f32[19,8,128]{2,1,0:T(8,128)S(1)}, u32[]{:S(2)}, u32[]{:S(2)}) collective-permute-start(f32[19,8,128]{2,1,0:T(8,128)S(1)} %select_add_fusion.refs_3_), channel_id=1, source_target_pairs={{0,2},{1,3},{2,0},{3,1},{4,6},{5,7},{6,4},{7,5},{8,10},{9,11},{10,... | collective-permute-start | bytes 233480 | tf_op jit(solution)/shard_map/ppermute | solution.py:345
  28.7 4.4 %collective-permute-start.9 = (f32[19,8,128]{2,1,0:T(8,128)S(1)}, f32[19,8,128]{2,1,0:T(8,128)S(1)}, u32[]{:S(2)}, u32[]{:S(2)}) collective-permute-start(f32[19,8,128]{2,1,0:T(8,128)S(1)} %select_add_fusion.refs_3_), channel_id=1, source_target_pairs={{0,1},{1,0},{2,3},{3,2},{4,5},{5,4},{6,7},{7,6},{8,9},{9,8},{10,11... | collective-permute-start | bytes 233480 | tf_op jit(solution)/shard_map/ppermute | solution.py:345
